TPU v7x, 256 devices: a whole 4x4x8 slice. The times are simulated.
256 devices in a mesh: row: 16 (over x, y_hi, core), col: 16 (over y_lo, z).
Axes of the slice: x: 4, y: 4 (y_hi: 2, y_lo: 2; y = y_hi * 2 + y_lo), z: 8, core: 2. Of those that a mesh axis runs over, the one named last changes fastest.
Arguments:
- iterate: float32 [96, 32, 128, 128], P('row', 'col'), may hold values from -1.2 to 1.2
- kept_cols: int32 [96, 32], P('row', 'col'), may hold values from 0 to 95, as said below
Outputs:
- square: float32 [96, 32, 128, 128], P('row', 'col')
- update: float32 [96, 32, 128, 128], P('row', 'col')
Inputs may be any that keep to these rules, and one draw needn't show every extreme that they name: kept_cols[i, s] lies among block columns g * 96 // 16 to (g + 1) * 96 // 16 - 1 with g = s // 2; the entries of one row are distinct, and every row keeps its own diagonal block i.
All inputs are finite; a program needn't handle non-finite values.
Results may differ from a plain program's by a relative error of at most 0.0003.
Values sent between devices are 32-bit elements; how exact they have to be, the bound alone decides.
No kernel may reach another device: no remote copies, remote signals or barrier semaphores. Data moves between devices by JAX's collectives and lax.ppermute only.
A program may use at most 192 MiB of HBM per device.

v0:
```python
import jax
import jax.numpy as jnp
from jax import lax
from jax.sharding import PartitionSpec as P


def body(iterate, kept_cols):
    block_rows, slot_count, block_size, _ = iterate.shape
    panel_vals, panel_ids = (
        lax.all_gather(iterate, "row", axis=0, tiled=True),
        lax.all_gather(kept_cols, "row", axis=0, tiled=True),
    )
    panel_width = panel_vals.shape[1]

    def contract(running, left_vals, left_ids):
        piece_len = left_ids.shape[1]
        partners = jnp.take(panel_vals, left_ids, axis=0)
        partner_ids = jnp.take(panel_ids, left_ids, axis=0)
        products = jnp.einsum(
            "itab,itobc->itoac",
            left_vals,
            partners,
            precision=lax.Precision.HIGHEST,
            preferred_element_type=jnp.float32,
        )
        products = products.reshape(block_rows, piece_len * panel_width, block_size * block_size)
        matches = (partner_ids[:, None, :, :] == kept_cols[:, :, None, None]).astype(jnp.float32)
        matches = matches.reshape(block_rows, slot_count, piece_len * panel_width)
        routed = jnp.einsum(
            "isk,ikm->ism",
            matches,
            products,
            precision=lax.Precision.HIGHEST,
            preferred_element_type=jnp.float32,
        )
        return running + routed.reshape(block_rows, slot_count, block_size, block_size)

    zeroed = jnp.zeros((block_rows, slot_count, block_size, block_size), jnp.float32)
    row_vals, row_ids = (
        lax.all_gather(iterate, "col", axis=1, tiled=True),
        lax.all_gather(kept_cols, "col", axis=1, tiled=True),
    )

    def step_group(groups, running):
        first_slot = groups * slot_count
        part_vals = lax.dynamic_slice_in_dim(row_vals, first_slot, slot_count, 1)
        part_ids = lax.dynamic_slice_in_dim(row_ids, first_slot, slot_count, 1)
        return contract(running, part_vals, part_ids)

    square = lax.fori_loop(0, row_ids.shape[1] // slot_count, step_group, zeroed)
    update = 1.5 * iterate - 0.5 * square
    return (square, update)


def solution(mesh):
    in_specs = (P("row", "col", None, None), P("row", "col"))
    out_specs = (P("row", "col", None, None), P("row", "col", None, None))
    return jax.shard_map(body, mesh=mesh, in_specs=in_specs, out_specs=out_specs, check_vma=False)
```

profile of v0, /device:TPU:1, one launch (start us, length us, event | category | flops | bytes accessed | tf_op | source)
XLA Modules:
  0.0 528.8 jit_solution(2920774422827009864)
XLA Ops:
  8.8 25.6 %all-gather.1 = s32[16,6,2]{1,2,0:T(2,128)S(1)} all-gather(s32[1,6,2]{1,2,0:T(2,128)S(1)} %bitcast.36), channel_id=1, replica_groups=mesh['row'=16,'col'=16] {'row'}, dimensions={0}, use_global_device_ids=true | all-gather | bytes 816 | tf_op jit(solution)/shard_map/all_gather | solution.py:11
  34.6 28.8 %all-gather = s32[16,2,6]{2,1,0:T(2,128)S(1)} all-gather(s32[1,2,6]{2,1,0:T(2,128)S(1)} %bitcast.37), channel_id=1, replica_groups=mesh['row'=16,'col'=16] {'col'}, dimensions={0}, use_global_device_ids=true | all-gather | bytes 816 | tf_op jit(solution)/shard_map/all_gather | solution.py:41
  63.4 47.5 %all-gather.5.cloned.1.call-done = f32[96,2,128,128]{3,2,1,0:T(8,128)} async-done(((f32[6,2,128,128]{3,2,1,0:T(8,128)}), f32[96,2,128,128]{3,2,1,0:T(8,128)}) %all-gather.5.cloned.1.call-update) | async-done | bytes 12582928 | tf_op jit(solution)/shard_map/all_gather | solution.py:10
  111.0 142.3 %all-gather.7.cloned.1.call-done = f32[6,32,128,128]{3,2,1,0:T(8,128)} async-done(((f32[6,2,128,128]{3,2,1,0:T(8,128)}), f32[6,32,128,128]{3,2,1,0:T(8,128)}) %all-gather.7.cloned.1.call-update) | async-done | bytes 12582928 | tf_op jit(solution)/shard_map/all_gather | solution.py:40
  253.3 266.3 %while.14 = (s32[]{:T(128)}, f32[6,2,128,128]{3,2,1,0:T(8,128)}, s32[6,32]{1,0:T(8,128)S(1)}, s32[96,2]{1,0:T(8,128)S(1)}, s32[6,2]{1,0:T(8,128)S(1)}, /*index=5...) while((s32[]{:T(128)}, f32[6,2,128,128]{3,2,1,0:T(8,128)}, ...), condition=%wide.region_1.0_spmd.clone, body=%wide.region_0.1_spmd.clone.sunk | while | flops 614204544 | bytes 29103976 | solution.py:50
  253.5 5.2 gather_fusion
  259.2 2.7 fusion.26
  270.1 5.2 gather_fusion
  286.8 5.2 gather_fusion
  292.5 2.7 fusion.26
  303.4 5.2 gather_fusion
  309.1 2.7 fusion.26
  320.1 5.2 gather_fusion
  325.8 2.7 fusion.26
  336.7 5.2 gather_fusion
  342.4 2.7 fusion.26
  353.3 5.2 gather_fusion
  359.0 2.7 fusion.26
  370.0 5.2 gather_fusion
  375.7 2.7 fusion.26
  386.6 5.2 gather_fusion
  403.3 5.2 gather_fusion
  409.0 2.7 fusion.26
  419.9 5.2 gather_fusion
  436.6 5.2 gather_fusion
  442.3 2.7 fusion.26
  453.2 5.2 gather_fusion
  469.8 5.2 gather_fusion
  475.6 2.7 fusion.26
  486.5 5.2 gather_fusion
  503.1 5.2 gather_fusion
  508.8 2.7 fusion.26
  (322 shorter events, 155.6 us)
Async XLA Ops:
  7.2 1.5 copy-start.2
  7.2 103.8 %all-gather.5.cloned.1.call-start = ((), (), s32[]{:S(2)}) async-start(), calls=%async_computation | async-start | bytes 13369344 | tf_op jit(solution)/shard_map/all_gather | solution.py:10
  7.9 245.4 %all-gather.7.cloned.1.call-start = ((), (), s32[]{:S(2)}) async-start(), calls=%async_computation.1 | async-start | bytes 13369344 | tf_op jit(solution)/shard_map/all_gather | solution.py:40
  266.5 2.3 copy-start
  269.1 0.9 copy-start.1
  283.1 2.3 copy-start
  285.7 0.9 copy-start.1
  299.8 2.3 copy-start
  302.4 0.9 copy-start.1
  316.4 2.3 copy-start
  319.0 0.9 copy-start.1
  333.0 2.3 copy-start
  335.6 0.9 copy-start.1
  349.7 2.3 copy-start
  352.3 0.9 copy-start.1
  366.3 2.3 copy-start
  368.9 0.9 copy-start.1
  383.0 2.3 copy-start
  385.6 0.9 copy-start.1
  399.6 2.3 copy-start
  402.2 0.9 copy-start.1
  416.3 2.3 copy-start
  418.9 0.9 copy-start.1
  432.9 2.3 copy-start
  435.5 0.9 copy-start.1
  449.6 2.3 copy-start
  452.2 0.9 copy-start.1
  466.2 2.3 copy-start
  482.8 2.3 copy-start
  485.4 0.9 copy-start.1
  499.5 2.3 copy-start
  516.1 2.3 copy-start
  (3 other events, 2.6 us)
Sparse Core Ops, SparseCore 0:
  10.7 100.2 all-gather.4
  112.8 140.4 all-gather.6
where the time goes:
time: 531 us; the launch traced here: 529 us
  waiting for transfers between devices  191 us (36%)
  local copies, waits for them, and re-layouts  190 us (36%)
  matrix products  69.4 us (13%)
  blocking collectives  54.4 us (10%)
  between operations  14.1 us (3%)
  other arithmetic  8.03 us (2%)
    all_gather x1, waiting for transfers between devices, body(): lax.all_gather(iterate, 'col', axis=1, tiled=True)  142 us
    gather x32, local copies, waits for them, and re-layouts, contract(): partners = jnp.take(panel_vals, left_ids, axis=0)  91 us
    all_gather x1, waiting for transfers between devices, body(): lax.all_gather(iterate, 'row', axis=0, tiled=True)  47.5 us
    dot_general x16, matrix products, contract(): jnp.einsum('itab,itobc->itoac', left_vals, partners, precision=lax.Precis...  43.5 us
    reshape x16, local copies, waits for them, and re-layouts, contract(): products.reshape(block_rows, piece_len * panel_width, block_size * block_...  31.2 us
    all_gather x1, blocking collectives, body(): lax.all_gather(kept_cols, 'col', axis=1, tiled=True)  28.8 us
    transpose x16, local copies, waits for them, and re-layouts, contract(): jnp.einsum('itab,itobc->itoac', left_vals, partners, precision=lax.Precis...  26.7 us
    dot_general x16, matrix products, contract(): jnp.einsum('isk,ikm->ism', matches, products, precision=lax.Precision.HIG...  26 us
  transfers between devices with their start and end apart: 2, of which 2 were waited for; matrix products, arithmetic and copies ran while one was open for 0% of the time, Pallas kernels for 0%

commit v1 on v0

v1 whole, which is shorter than its diff:
```python
import functools

import jax
import jax.numpy as jnp
import numpy as np
from jax import lax
from jax.experimental import pallas as pl
from jax.experimental.pallas import tpu as pltpu
from jax.sharding import PartitionSpec as P

AXES = ("row", "col")
BS = 128
ROWS = 6
BLOCKS = 12
SHARD = BLOCKS * BS
UNROLL = 4
MAX_PAIRS = 96 + 2 * UNROLL


def device_id(x, y, z, c):
    return ((x * 2 + y // 2) * 2 + c) * 16 + (y % 2) * 8 + z


def table(move, keep=lambda x, y, z, c: True):
    pairs = []
    for x in range(4):
        for y in range(4):
            for z in range(8):
                for c in range(2):
                    if keep(x, y, z, c):
                        tx, ty, tz, tc = move(x, y, z, c)
                        pairs.append((device_id(x, y, z, c), device_id(tx % 4, ty % 4, tz % 8, tc)))
    return pairs


def near(x, y, z, c):
    return x // 2 == y % 2


IN_PAIR = table(lambda x, y, z, c: (x ^ 1, y, z, c))
CROSS = table(lambda x, y, z, c: (3 - x, y, z, c))
CROSS_NEAR = table(lambda x, y, z, c: (3 - x, y, z, c), near)
Y_FAR_NEAR = table(lambda x, y, z, c: (x, y + 2, z, c), near)
Y_UP = table(lambda x, y, z, c: (x, y + 1, z, c))
Y_DOWN = table(lambda x, y, z, c: (x, y - 1, z, c))
Y_LO = table(lambda x, y, z, c: (x, y ^ 1, z, c))
CORE = table(lambda x, y, z, c: (x, y, z, 1 - c))
Z_GROUPS = [[g * 8 + z for z in range(8)] for g in range(2)]


def send(value, pairs):
    return lax.ppermute(value, AXES, pairs)


def kernel(ids, slots, left, *refs):
    right = refs[:8]
    out = refs[8]
    lbuf, rbuf, acc, pl_l, pl_r, pl_o, lsem, rsem = refs[9:]
    first_k = slots[8]

    for q in range(8):
        pltpu.make_async_copy(left.at[q, pl.ds(0, SHARD), :], lbuf.at[pl.ds(q * SHARD, SHARD), :], lsem).start()
    for n in range(8):
        at = pl.multiple_of(slots[n] * SHARD, SHARD)
        pltpu.make_async_copy(right[n].at[pl.ds(0, SHARD), :], rbuf.at[pl.ds(at, SHARD), :], rsem).start()

    zero_block = 8 * BLOCKS
    rbuf[pl.ds(zero_block * BS, BS), :] = jnp.zeros((BS, BS), jnp.float32)
    acc[...] = jnp.zeros_like(acc)

    def list_output(o, n):
        i = o // 2
        j = ids[16 * 16 + o]
        for q in range(8):
            for t in range(2):
                lb = q * BLOCKS + i * 2 + t
                k = ids[q * 16 + i * 2 + t] - (first_k + q * ROWS)
                at = (8 + q) * 16 + k * 2
                m1 = (ids[at + 1] == j).astype(jnp.int32)
                m0 = (ids[at] == j).astype(jnp.int32)
                pl_l[n] = lb
                pl_r[n] = q * BLOCKS + k * 2 + m1
                pl_o[n // 2] = o
                n = n + m0 + m1
        pl_l[n] = 0
        pl_r[n] = zero_block
        return n + n % 2

    n = lax.fori_loop(0, BLOCKS, list_output, 0)
    pairs = n // 2
    for u in range(UNROLL):
        pl_o[pairs + u] = BLOCKS
        for h in range(2):
            pl_l[n + 2 * u + h] = 0
            pl_r[n + 2 * u + h] = zero_block

    for q in range(8):
        pltpu.make_async_copy(left.at[q, pl.ds(0, SHARD), :], lbuf.at[pl.ds(q * SHARD, SHARD), :], lsem).wait()
        pltpu.make_async_copy(right[q].at[pl.ds(0, SHARD), :], rbuf.at[pl.ds(q * SHARD, SHARD), :], rsem).wait()

    def split(a):
        hi = a.astype(jnp.bfloat16)
        return hi, (a - hi.astype(jnp.float32)).astype(jnp.bfloat16)

    def block(buf, b):
        return buf[pl.ds(pl.multiple_of(b * BS, BS), BS), :]

    def step(s, carry):
        results = []
        for u in range(UNROLL):
            e = s * UNROLL + u
            a = jnp.concatenate([block(lbuf, pl_l[2 * e]), block(lbuf, pl_l[2 * e + 1])], axis=1)
            b = jnp.concatenate([block(rbuf, pl_r[2 * e]), block(rbuf, pl_r[2 * e + 1])], axis=0)
            a = jnp.concatenate(split(a), axis=0)
            b = jnp.concatenate(split(b), axis=1)
            r = jnp.dot(a, b, preferred_element_type=jnp.float32)
            results.append(r[:BS, :BS] + (r[:BS, BS:] + r[BS:, :BS]) + r[BS:, BS:])
        for u in range(UNROLL):
            o = pl_o[s * UNROLL + u]
            acc[o] = acc[o] + results[u]
        return carry

    lax.fori_loop(0, (pairs + UNROLL - 1) // UNROLL, step, 0)
    out[...] = acc[:BLOCKS]


def contract(ids, slots, left, right):
    return pl.pallas_call(
        kernel,
        out_shape=jax.ShapeDtypeStruct((BLOCKS, BS, BS), jnp.float32),
        in_specs=[pl.BlockSpec(memory_space=pltpu.SMEM)] * 2 + [pl.BlockSpec(memory_space=pl.ANY)] * 9,
        out_specs=pl.BlockSpec(memory_space=pltpu.VMEM),
        scratch_shapes=[
            pltpu.VMEM((8 * SHARD, BS), jnp.float32),
            pltpu.VMEM((8 * SHARD + BS, BS), jnp.float32),
            pltpu.VMEM((BLOCKS + 1, BS, BS), jnp.float32),
            pltpu.SMEM((2 * MAX_PAIRS + 2,), jnp.int32),
            pltpu.SMEM((2 * MAX_PAIRS + 2,), jnp.int32),
            pltpu.SMEM((MAX_PAIRS + 1,), jnp.int32),
            pltpu.SemaphoreType.DMA,
            pltpu.SemaphoreType.DMA,
        ],
        compiler_params=pltpu.CompilerParams(vmem_limit_bytes=40 * 2 ** 20),
        cost_estimate=pl.CostEstimate(flops=3 * 10 ** 9, bytes_accessed=13 * 10 ** 6, transcendentals=0),
    )(ids, slots, left, *right)


def body(iterate, kept_cols):
    row, col = lax.axis_index("row"), lax.axis_index("col")
    x, y_hi, core = row // 4, (row // 2) % 2, row % 2
    y_lo, z = col // 8, col % 8
    is_near = (x // 2) == y_lo
    first_x = jnp.where(is_near, x, 3 - x)

    ids8 = jnp.pad(kept_cols.reshape(1, BLOCKS).astype(jnp.float32), ((0, 7), (0, BS - BLOCKS)))
    own = jnp.concatenate([iterate.reshape(SHARD, BS), ids8], axis=0)

    left = lax.all_gather(own, "col", axis=0, tiled=False, axis_index_groups=Z_GROUPS)
    partner_ids = send(ids8, Y_LO)

    half = SHARD // 2
    in_pair, cross = send(own, IN_PAIR), send(own, CROSS)
    far = send(own, Y_FAR_NEAR)
    far_cross = send(far, CROSS_NEAR)
    nb1 = jnp.where(is_near, cross, own)
    up1, down1 = send(nb1, Y_UP), send(nb1, Y_DOWN)
    diag = jnp.concatenate([send(in_pair[:half], CROSS), send(cross[half:], IN_PAIR)], axis=0)
    far1 = jnp.where(is_near, far, far_cross)
    far2 = send(far1, IN_PAIR)
    nb2 = jnp.where(is_near, diag, in_pair)
    up2, down2 = send(nb2, Y_UP), send(nb2, Y_DOWN)
    here1 = jnp.where(is_near, own, cross)
    here2 = jnp.where(is_near, in_pair, diag)

    def both_cores(parts):
        return parts + [send(v, CORE) for v in parts]

    def slots_of(x_bits, y_his):
        local = [xb % 2 * 4 + yh * 2 for xb, yh in zip(x_bits, y_his)]
        slots = [s + core for s in local] + [s + 1 - core for s in local]
        return jnp.stack(slots + [y_lo * 48]).astype(jnp.int32)

    def ids_of(parts, slots, out_ids):
        rows = jnp.stack([v[SHARD, :16] for v in parts])
        rows = jnp.zeros((8, 16), jnp.float32).at[slots[:8]].set(rows, unique_indices=True)
        rows = jnp.concatenate([left[:, SHARD, :16], rows, out_ids[:1, :16]], axis=0)
        return rows.astype(jnp.int32).reshape(-1)

    y = y_hi * 2 + y_lo
    below, above = (y - 1) % 4 // 2, (y + 1) % 4 // 2
    parts = both_cores([up1, down1, up2, down2])
    slots = slots_of([first_x, first_x, first_x + 1, first_x + 1], [below, above, below, above])
    partial = contract(ids_of(parts, slots, partner_ids), slots, left, parts)
    received = send(partial, Y_LO)

    parts = both_cores([here1, here2, far1, far2])
    slots = slots_of([first_x, first_x + 1, first_x, first_x + 1], [y_hi, y_hi, 1 - y_hi, 1 - y_hi])
    mine = contract(ids_of(parts, slots, ids8), slots, left, parts)

    square = (mine + received).reshape(iterate.shape)
    update = 1.5 * iterate - 0.5 * square
    return (square, update)


def solution(mesh):
    in_specs = (P("row", "col", None, None), P("row", "col"))
    out_specs = (P("row", "col", None, None), P("row", "col", None, None))
    return jax.shard_map(body, mesh=mesh, in_specs=in_specs, out_specs=out_specs, check_vma=False)
```

time: 531 us -> 140 us (0.26)
  local copies, waits for them, and re-layouts: 190 us -> 18.9 us
  waiting for transfers between devices: 191 us -> 42.1 us
  matrix products: 69.4 us -> 0 us
  blocking collectives: 54.4 us -> 0 us
  starting transfers between devices: 0.08 us -> 40.3 us
  Pallas kernels: 0 us -> 15.2 us
    all_gather x2 -> x1, waiting for transfers between devices: 190 us -> 0.02 us  [body(): lax.all_gather(own, 'col', axis=0, tiled=False, axis_index_groups=Z_GROUPS)]
    gather x80 -> x0, local copies, waits for them, and re-layouts: 103 us -> none  [the longest x32 91 us: contract(): partners = jnp.take(panel_vals, left_ids, axis=0)]
    dot_general x32 -> x0, matrix products: 69.4 us -> none  [the longest x16 43.5 us: contract(): jnp.einsum('itab,itobc->itoac', left_vals, partners, precision=lax.Precis...]
    all_gather x2 -> x0, blocking collectives: 54.4 us -> none  [the longest x1 28.8 us: body(): lax.all_gather(kept_cols, 'col', axis=1, tiled=True)]
    reshape x32 -> x0, local copies, waits for them, and re-layouts: 42 us -> none  [the longest x16 31.2 us: contract(): products.reshape(block_rows, piece_len * panel_width, block_size * block_...]
    ppermute x0 -> x21, waiting for transfers between devices: none -> 42 us  [send(): return lax.ppermute(value, AXES, pairs)]
    ppermute x0 -> x21, starting transfers between devices: none -> 40.3 us  [send(): return lax.ppermute(value, AXES, pairs)]
    transpose x16 -> x0, local copies, waits for them, and re-layouts: 26.7 us -> none  [contract(): jnp.einsum('itab,itobc->itoac', left_vals, partners, precision=lax.Precis...]
  transfers between devices with their start and end apart: 2 -> 22, of which waited for: 2 -> 7; matrix products, arithmetic and copies ran while one was open for 0% -> 9% of each run, Pallas kernels for 0% -> 5%
where the time goes in v1:
time: 140 us; the launch traced here: 139 us
  waiting for transfers between devices  42.1 us (30%)
  starting transfers between devices  40.3 us (29%)
  local copies, waits for them, and re-layouts  18.9 us (13%)
  Pallas kernels  15.2 us (11%)
  between operations  14.3 us (10%)
  other arithmetic  7.73 us (6%)
    ppermute x21, waiting for transfers between devices, send(): return lax.ppermute(value, AXES, pairs)  42 us
    ppermute x21, starting transfers between devices, send(): return lax.ppermute(value, AXES, pairs)  40.3 us
    pallas_call x2, Pallas kernels, contract(): pl.pallas_call(kernel, out_shape=jax.ShapeDtypeStruct((BLOCKS, BS, BS), j...  15.2 us
    slice x16, local copies, waits for them, and re-layouts, ids_of(): rows = jnp.stack([v[SHARD, :16] for v in parts])  8.13 us
    unnamed x17, local copies, waits for them, and re-layouts  8.01 us
  transfers between devices with their start and end apart: 22, of which 7 were waited for; matrix products, arithmetic and copies ran while one was open for 9% of the time, Pallas kernels for 5%

profile of v1, /device:TPU:1, one launch (start us, length us, event | category | flops | bytes accessed | tf_op | source)
XLA Modules:
  0.0 138.6 jit_solution(11691630624210647992)
XLA Ops:
  7.2 0.7 convert_element_type.30
  8.1 2.1 %pad_maximum_fusion = f32[1544,128]{1,0:T(8,128)} fusion(f32[8,128]{1,0:T(8,128)S(1)} %pad.4, f32[1536,128]{1,0:T(8,128)} %bitcast.46), kind=kLoop, calls=%fused_computation.2 | loop fusion | flops 197632 | bytes 1581056 | tf_op jit(solution)/shard_map/concatenate | solution.py:156
  10.2 2.1 %collective-permute-start.1 = (f32[1544,128]{1,0:T(8,128)}, f32[1544,128]{1,0:T(8,128)S(1)}, u32[]{:S(2)}, u32[]{:S(2)}) collective-permute-start(f32[1544,128]{1,0:T(8,128)} %pad_maximum_fusion), channel_id=1, source_target_pairs={{0,64},{16,80},{1,65},{17,81},{2,66},{18,82},{3,67},{19,83},{4,68}... | collective-permute-start | bytes 2371592 | tf_op jit(solution)/shard_map/ppermute | solution.py:52
  12.3 1.8 %collective-permute-start = (f32[1544,128]{1,0:T(8,128)}, f32[1544,128]{1,0:T(8,128)S(1)}, u32[]{:S(2)}, u32[]{:S(2)}) collective-permute-start(f32[1544,128]{1,0:T(8,128)} %pad_maximum_fusion), channel_id=1, source_target_pairs={{0,192},{16,208},{1,193},{17,209},{2,194},{18,210},{3,195},{19,211... | collective-permute-start | bytes 2371592 | tf_op jit(solution)/shard_map/ppermute | solution.py:52
  14.1 4.8 %collective-permute-start.4 = (f32[1544,128]{1,0:T(8,128)}, f32[1544,128]{1,0:T(8,128)}, u32[]{:S(2)}, u32[]{:S(2)}) collective-permute-start(f32[1544,128]{1,0:T(8,128)} %pad_maximum_fusion), channel_id=1, source_target_pairs={{0,32},{16,48},{1,33},{17,49},{2,34},{18,50},{3,35},{19,51},{4,36}... | collective-permute-start | bytes 2371592 | tf_op jit(solution)/shard_map/ppermute | solution.py:52
  19.1 9.5 %collective-permute-done.1 = f32[1544,128]{1,0:T(8,128)S(1)} collective-permute-done((f32[1544,128]{1,0:T(8,128)}, f32[1544,128]{1,0:T(8,128)S(1)}, u32[]{:S(2)}, u32[]{:S(2)}) %collective-permute-start.1) | collective-permute-done | bytes 790560 | tf_op jit(solution)/shard_map/ppermute | solution.py:52
  28.7 3.8 %collective-permute-start.2 = (f32[768,128]{1,0:T(8,128)S(1)}, f32[768,128]{1,0:T(8,128)S(1)}, u32[]{:S(2)}, u32[]{:S(2)}) collective-permute-start(f32[768,128]{1,0:T(8,128)S(1)} %slice.91), channel_id=1, source_target_pairs={{0,192},{16,208},{1,193},{17,209},{2,194},{18,210},{3,195},{19,211... | collective-permute-start | bytes 1179656 | tf_op jit(solution)/shard_map/ppermute | solution.py:52
  32.6 1.2 broadcast_select_fusion.1
  33.9 2.8 %collective-permute-start.12 = (f32[1544,128]{1,0:T(8,128)S(1)}, f32[1544,128]{1,0:T(8,128)}, u32[]{:S(2)}, u32[]{:S(2)}) collective-permute-start(f32[1544,128]{1,0:T(8,128)S(1)} %get-tuple-element.4), channel_id=1, source_target_pairs={{0,40},{16,56},{1,41},{17,57},{2,42},{18,58},{3,43},{19,59},{4,44}... | collective-permute-start | bytes 2371592 | tf_op jit(solution)/shard_map/ppermute | solution.py:52
  36.7 3.7 %collective-permute-done.2 = f32[768,128]{1,0:T(8,128)S(1)} collective-permute-done((f32[768,128]{1,0:T(8,128)S(1)}, f32[768,128]{1,0:T(8,128)S(1)}, u32[]{:S(2)}, u32[]{:S(2)}) %collective-permute-start.2) | collective-permute-done | bytes 393248 | tf_op jit(solution)/shard_map/ppermute | solution.py:52
  40.4 4.6 %collective-permute-start.5 = (f32[1544,128]{1,0:T(8,128)}, f32[1544,128]{1,0:T(8,128)S(1)}, u32[]{:S(2)}, u32[]{:S(2)}) collective-permute-start(f32[1544,128]{1,0:T(8,128)} %collective-permute-done.4), channel_id=1, source_target_pairs={{0,192},{16,208},{1,193},{17,209},{2,194},{18,210},{3,195},{19,211... | collective-permute-start | bytes 2371592 | tf_op jit(solution)/shard_map/ppermute | solution.py:52
  45.0 2.6 %collective-permute-start.7 = (f32[1544,128]{1,0:T(8,128)S(1)}, f32[1544,128]{1,0:T(8,128)S(1)}, u32[]{:S(2)}, u32[]{:S(2)}) collective-permute-start(f32[1544,128]{1,0:T(8,128)S(1)} %get-tuple-element.5.refs_0_), channel_id=1, source_target_pairs={{0,16},{16,0},{1,17},{17,1},{2,18},{18,2},{3,19},{19,3},{4,20},{20... | collective-permute-start | bytes 2371592 | tf_op jit(solution)/shard_map/ppermute | solution.py:52
  47.8 12.1 %collective-permute-done.5 = f32[1544,128]{1,0:T(8,128)S(1)} collective-permute-done((f32[1544,128]{1,0:T(8,128)}, f32[1544,128]{1,0:T(8,128)S(1)}, u32[]{:S(2)}, u32[]{:S(2)}) %collective-permute-start.5) | collective-permute-done | bytes 790560 | tf_op jit(solution)/shard_map/ppermute | solution.py:52
  59.9 3.7 %collective-permute-start.14 = (f32[1544,128]{1,0:T(8,128)S(1)}, f32[1544,128]{1,0:T(8,128)}, u32[]{:S(2)}, u32[]{:S(2)}) collective-permute-start(f32[1544,128]{1,0:T(8,128)S(1)} %get-tuple-element.2), channel_id=1, source_target_pairs={{0,40},{16,56},{1,41},{17,57},{2,42},{18,58},{3,43},{19,59},{4,44}... | collective-permute-start | bytes 2371592 | tf_op jit(solution)/shard_map/ppermute | solution.py:52
  63.5 1.2 broadcast_select_fusion.2.refs_2_
  64.9 3.4 %collective-permute-start.8 = (f32[1544,128]{1,0:T(8,128)S(1)}, f32[1544,128]{1,0:T(8,128)S(1)}, u32[]{:S(2)}, u32[]{:S(2)}) collective-permute-start(f32[1544,128]{1,0:T(8,128)S(1)} %get-tuple-element.3.refs_1_), channel_id=1, source_target_pairs={{0,16},{16,0},{1,17},{17,1},{2,18},{18,2},{3,19},{19,3},{4,20},{20... | collective-permute-start | bytes 2371592 | tf_op jit(solution)/shard_map/ppermute | solution.py:52
  68.4 8.9 %collective-permute-done.14.refs_3_ = f32[1544,128]{1,0:T(8,128)} collective-permute-done((f32[1544,128]{1,0:T(8,128)S(1)}, f32[1544,128]{1,0:T(8,128)}, u32[]{:S(2)}, u32[]{:S(2)}) %collective-permute-start.14) | collective-permute-done | bytes 790560 | tf_op jit(solution)/shard_map/ppermute | solution.py:52
  77.4 4.0 %collective-permute-start.16 = (f32[1544,128]{1,0:T(8,128)}, f32[1544,128]{1,0:T(8,128)}, u32[]{:S(2)}, u32[]{:S(2)}) collective-permute-start(f32[1544,128]{1,0:T(8,128)} %collective-permute-done.12.refs_1_), channel_id=1, source_target_pairs={{0,16},{16,0},{1,17},{17,1},{2,18},{18,2},{3,19},{19,3},{4,20},{20... | collective-permute-start | bytes 2371592 | tf_op jit(solution)/shard_map/ppermute | solution.py:52
  81.9 4.3 %collective-permute-start.15 = (f32[1544,128]{1,0:T(8,128)}, f32[1544,128]{1,0:T(8,128)}, u32[]{:S(2)}, u32[]{:S(2)}) collective-permute-start(f32[1544,128]{1,0:T(8,128)} %collective-permute-done.11.refs_0_), channel_id=1, source_target_pairs={{0,16},{16,0},{1,17},{17,1},{2,18},{18,2},{3,19},{19,3},{4,20},{20... | collective-permute-start | bytes 2371592 | tf_op jit(solution)/shard_map/ppermute | solution.py:52
  87.4 1.1 collective-permute-start.10
  89.6 0.7 slice.100
  97.0 0.7 slice.99
  98.4 0.8 slice.89
  99.2 2.8 %copy-done = f32[12352,128]{1,0:T(8,128)S(1)} copy-done((f32[12352,128]{1,0:T(8,128)S(1)}, f32[12352,128]{1,0:T(8,128)}, u32[]{:S(2)}) %copy-start) | copy-done | bytes 6324248
  102.0 7.9 %shard_map.42 = f32[12,128,128]{2,1,0:T(8,128)} custom-call(s32[272]{0:T(512)S(1)} %convert_element_type.35.ids, s32[9]{0:T(128)S(1)} %stack.138.slots, f32[8,1544,128]{2,1,0:T(8,128)S(1)} %bitcast.44, f32[1544,128]{1,0:T(8,128)} %collective-permute-done.11.refs_0_, f32[1544,128]{1,0:T(8,128)} %collective-permute-done.12.refs_1_, ...), custom_call_target="tpu_custom_call" | custom-call | flops 3000000000 | bytes 13000000 | tf_op jit(solution)/shard_map/pallas_call | solution.py:128
  110.4 2.8 %copy-done.1 = f32[12352,128]{1,0:T(8,128)S(1)} copy-done((f32[12352,128]{1,0:T(8,128)S(1)}, f32[12352,128]{1,0:T(8,128)}, u32[]{:S(2)}) %copy-start.1) | copy-done | bytes 6324248
  113.2 1.1 copy-done.3
  114.4 1.1 copy-done.5
  115.5 7.3 %shard_map.41 = f32[12,128,128]{2,1,0:T(8,128)S(1)} custom-call(s32[272]{0:T(512)S(1)} %convert_element_type.33.ids, s32[9]{0:T(128)S(1)} %stack.119.slots, f32[8,1544,128]{2,1,0:T(8,128)S(1)} %bitcast.45, f32[1544,128]{1,0:T(8,128)S(1)} %get-tuple-element.5.refs_0_, f32[1544,128]{1,0:T(8,128)S(1)} %get-tuple-element.3.refs_1_, ...), custom_call_target="tpu_custom_call" | custom-call | flops 3000000000 | bytes 13000000 | tf_op jit(solution)/shard_map/pallas_call | solution.py:128
  122.8 6.6 %collective-permute-done.20 = f32[12,128,128]{2,1,0:T(8,128)} collective-permute-done((f32[12,128,128]{2,1,0:T(8,128)}, f32[12,128,128]{2,1,0:T(8,128)}, u32[]{:S(2)}, u32[]{:S(2)}) %collective-permute-start.20) | collective-permute-done | bytes 786464 | tf_op jit(solution)/shard_map/ppermute | solution.py:52
  129.3 1.2 add.176
  130.6 1.1 multiply_subtract_fusion
  (77 shorter events, 11.5 us)
Async XLA Ops:
  7.2 91.2 %all-gather.3.cloned.1.call-start = ((), (), s32[]{:S(2)}) async-start(), calls=%async_computation | async-start | bytes 7114752 | tf_op jit(solution)/shard_map/all_gather | solution.py:158
  10.2 18.5 %collective-permute-start.1 = (f32[1544,128]{1,0:T(8,128)}, f32[1544,128]{1,0:T(8,128)S(1)}, u32[]{:S(2)}, u32[]{:S(2)}) collective-permute-start(f32[1544,128]{1,0:T(8,128)} %pad_maximum_fusion), channel_id=1, source_target_pairs={{0,64},{16,80},{1,65},{17,81},{2,66},{18,82},{3,67},{19,83},{4,68}... | collective-permute-start | bytes 2371592 | tf_op jit(solution)/shard_map/ppermute | solution.py:52
  12.3 20.2 %collective-permute-start = (f32[1544,128]{1,0:T(8,128)}, f32[1544,128]{1,0:T(8,128)S(1)}, u32[]{:S(2)}, u32[]{:S(2)}) collective-permute-start(f32[1544,128]{1,0:T(8,128)} %pad_maximum_fusion), channel_id=1, source_target_pairs={{0,192},{16,208},{1,193},{17,209},{2,194},{18,210},{3,195},{19,211... | collective-permute-start | bytes 2371592 | tf_op jit(solution)/shard_map/ppermute | solution.py:52
  14.1 22.6 %collective-permute-start.4 = (f32[1544,128]{1,0:T(8,128)}, f32[1544,128]{1,0:T(8,128)}, u32[]{:S(2)}, u32[]{:S(2)}) collective-permute-start(f32[1544,128]{1,0:T(8,128)} %pad_maximum_fusion), channel_id=1, source_target_pairs={{0,32},{16,48},{1,33},{17,49},{2,34},{18,50},{3,35},{19,51},{4,36}... | collective-permute-start | bytes 2371592 | tf_op jit(solution)/shard_map/ppermute | solution.py:52
  18.9 45.8 %collective-permute-start.19 = (f32[8,128]{1,0:T(8,128)S(1)}, f32[8,128]{1,0:T(8,128)S(1)}, u32[]{:S(2)}, u32[]{:S(2)}) collective-permute-start(f32[8,128]{1,0:T(8,128)S(1)} %pad.4), channel_id=1, source_target_pairs={{0,8},{16,24},{1,9},{17,25},{2,10},{18,26},{3,11},{19,27},{4,12},{... | collective-permute-start | bytes 12296 | tf_op jit(solution)/shard_map/ppermute | solution.py:52
  28.7 11.7 %collective-permute-start.2 = (f32[768,128]{1,0:T(8,128)S(1)}, f32[768,128]{1,0:T(8,128)S(1)}, u32[]{:S(2)}, u32[]{:S(2)}) collective-permute-start(f32[768,128]{1,0:T(8,128)S(1)} %slice.91), channel_id=1, source_target_pairs={{0,192},{16,208},{1,193},{17,209},{2,194},{18,210},{3,195},{19,211... | collective-permute-start | bytes 1179656 | tf_op jit(solution)/shard_map/ppermute | solution.py:52
  32.5 12.4 %collective-permute-start.3 = (f32[776,128]{1,0:T(8,128)S(1)}, f32[776,128]{1,0:T(8,128)S(1)}, u32[]{:S(2)}, u32[]{:S(2)}) collective-permute-start(f32[776,128]{1,0:T(8,128)S(1)} %slice.92), channel_id=1, source_target_pairs={{0,64},{16,80},{1,65},{17,81},{2,66},{18,82},{3,67},{19,83},{4,68}... | collective-permute-start | bytes 1191944 | tf_op jit(solution)/shard_map/ppermute | solution.py:52
  33.9 31.0 %collective-permute-start.12 = (f32[1544,128]{1,0:T(8,128)S(1)}, f32[1544,128]{1,0:T(8,128)}, u32[]{:S(2)}, u32[]{:S(2)}) collective-permute-start(f32[1544,128]{1,0:T(8,128)S(1)} %get-tuple-element.4), channel_id=1, source_target_pairs={{0,40},{16,56},{1,41},{17,57},{2,42},{18,58},{3,43},{19,59},{4,44}... | collective-permute-start | bytes 2371592 | tf_op jit(solution)/shard_map/ppermute | solution.py:52
  36.7 31.6 %collective-permute-start.11 = (f32[1544,128]{1,0:T(8,128)S(1)}, f32[1544,128]{1,0:T(8,128)}, u32[]{:S(2)}, u32[]{:S(2)}) collective-permute-start(f32[1544,128]{1,0:T(8,128)S(1)} %get-tuple-element.4), channel_id=1, source_target_pairs={{0,8},{16,24},{1,9},{17,25},{2,10},{18,26},{3,11},{19,27},{4,12},{... | collective-permute-start | bytes 2371592 | tf_op jit(solution)/shard_map/ppermute | solution.py:52
  40.4 19.5 %collective-permute-start.5 = (f32[1544,128]{1,0:T(8,128)}, f32[1544,128]{1,0:T(8,128)S(1)}, u32[]{:S(2)}, u32[]{:S(2)}) collective-permute-start(f32[1544,128]{1,0:T(8,128)} %collective-permute-done.4), channel_id=1, source_target_pairs={{0,192},{16,208},{1,193},{17,209},{2,194},{18,210},{3,195},{19,211... | collective-permute-start | bytes 2371592 | tf_op jit(solution)/shard_map/ppermute | solution.py:52
  45.0 23.4 %collective-permute-start.7 = (f32[1544,128]{1,0:T(8,128)S(1)}, f32[1544,128]{1,0:T(8,128)S(1)}, u32[]{:S(2)}, u32[]{:S(2)}) collective-permute-start(f32[1544,128]{1,0:T(8,128)S(1)} %get-tuple-element.5.refs_0_), channel_id=1, source_target_pairs={{0,16},{16,0},{1,17},{17,1},{2,18},{18,2},{3,19},{19,3},{4,20},{20... | collective-permute-start | bytes 2371592 | tf_op jit(solution)/shard_map/ppermute | solution.py:52
  59.9 17.5 %collective-permute-start.14 = (f32[1544,128]{1,0:T(8,128)S(1)}, f32[1544,128]{1,0:T(8,128)}, u32[]{:S(2)}, u32[]{:S(2)}) collective-permute-start(f32[1544,128]{1,0:T(8,128)S(1)} %get-tuple-element.2), channel_id=1, source_target_pairs={{0,40},{16,56},{1,41},{17,57},{2,42},{18,58},{3,43},{19,59},{4,44}... | collective-permute-start | bytes 2371592 | tf_op jit(solution)/shard_map/ppermute | solution.py:52
  64.8 17.2 %collective-permute-start.13 = (f32[1544,128]{1,0:T(8,128)S(1)}, f32[1544,128]{1,0:T(8,128)}, u32[]{:S(2)}, u32[]{:S(2)}) collective-permute-start(f32[1544,128]{1,0:T(8,128)S(1)} %get-tuple-element.2), channel_id=1, source_target_pairs={{0,8},{16,24},{1,9},{17,25},{2,10},{18,26},{3,11},{19,27},{4,12},{... | collective-permute-start | bytes 2371592 | tf_op jit(solution)/shard_map/ppermute | solution.py:52
  64.9 21.3 %collective-permute-start.8 = (f32[1544,128]{1,0:T(8,128)S(1)}, f32[1544,128]{1,0:T(8,128)S(1)}, u32[]{:S(2)}, u32[]{:S(2)}) collective-permute-start(f32[1544,128]{1,0:T(8,128)S(1)} %get-tuple-element.3.refs_1_), channel_id=1, source_target_pairs={{0,16},{16,0},{1,17},{17,1},{2,18},{18,2},{3,19},{19,3},{4,20},{20... | collective-permute-start | bytes 2371592 | tf_op jit(solution)/shard_map/ppermute | solution.py:52
  68.3 18.0 %collective-permute-start.9 = (f32[1544,128]{1,0:T(8,128)S(1)}, f32[1544,128]{1,0:T(8,128)S(1)}, u32[]{:S(2)}, u32[]{:S(2)}) collective-permute-start(f32[1544,128]{1,0:T(8,128)S(1)} %broadcast_select_fusion.2.refs_2_), channel_id=1, source_target_pairs={{0,16},{16,0},{1,17},{17,1},{2,18},{18,2},{3,19},{19,3},{4,20},{20... | collective-permute-start | bytes 2371592 | tf_op jit(solution)/shard_map/ppermute | solution.py:52
  68.4 18.9 %collective-permute-start.6 = (f32[1544,128]{1,0:T(8,128)S(1)}, f32[1544,128]{1,0:T(8,128)}, u32[]{:S(2)}, u32[]{:S(2)}) collective-permute-start(f32[1544,128]{1,0:T(8,128)S(1)} %broadcast_select_fusion.2.refs_2_), channel_id=1, source_target_pairs={{0,64},{16,80},{1,65},{17,81},{2,66},{18,82},{3,67},{19,83},{4,68}... | collective-permute-start | bytes 2371592 | tf_op jit(solution)/shard_map/ppermute | solution.py:52
  77.4 16.3 %collective-permute-start.16 = (f32[1544,128]{1,0:T(8,128)}, f32[1544,128]{1,0:T(8,128)}, u32[]{:S(2)}, u32[]{:S(2)}) collective-permute-start(f32[1544,128]{1,0:T(8,128)} %collective-permute-done.12.refs_1_), channel_id=1, source_target_pairs={{0,16},{16,0},{1,17},{17,1},{2,18},{18,2},{3,19},{19,3},{4,20},{20... | collective-permute-start | bytes 2371592 | tf_op jit(solution)/shard_map/ppermute | solution.py:52
  81.9 12.4 %collective-permute-start.15 = (f32[1544,128]{1,0:T(8,128)}, f32[1544,128]{1,0:T(8,128)}, u32[]{:S(2)}, u32[]{:S(2)}) collective-permute-start(f32[1544,128]{1,0:T(8,128)} %collective-permute-done.11.refs_0_), channel_id=1, source_target_pairs={{0,16},{16,0},{1,17},{17,1},{2,18},{18,2},{3,19},{19,3},{4,20},{20... | collective-permute-start | bytes 2371592 | tf_op jit(solution)/shard_map/ppermute | solution.py:52
  86.2 1.1 copy-start.2
  86.2 8.8 %collective-permute-start.18 = (f32[1544,128]{1,0:T(8,128)}, f32[1544,128]{1,0:T(8,128)}, u32[]{:S(2)}, u32[]{:S(2)}) collective-permute-start(f32[1544,128]{1,0:T(8,128)} %collective-permute-done.14.refs_3_), channel_id=1, source_target_pairs={{0,16},{16,0},{1,17},{17,1},{2,18},{18,2},{3,19},{19,3},{4,20},{20... | collective-permute-start | bytes 2371592 | tf_op jit(solution)/shard_map/ppermute | solution.py:52
  86.3 1.1 copy-start.4
  86.3 9.4 %collective-permute-start.17 = (f32[1544,128]{1,0:T(8,128)}, f32[1544,128]{1,0:T(8,128)}, u32[]{:S(2)}, u32[]{:S(2)}) collective-permute-start(f32[1544,128]{1,0:T(8,128)} %collective-permute-done.13.refs_2_), channel_id=1, source_target_pairs={{0,16},{16,0},{1,17},{17,1},{2,18},{18,2},{3,19},{19,3},{4,20},{20... | collective-permute-start | bytes 2371592 | tf_op jit(solution)/shard_map/ppermute | solution.py:52
  87.4 9.6 %collective-permute-start.10 = (f32[1544,128]{1,0:T(8,128)}, f32[1544,128]{1,0:T(8,128)}, u32[]{:S(2)}, u32[]{:S(2)}) collective-permute-start(f32[1544,128]{1,0:T(8,128)} %collective-permute-done.6.refs_3_), channel_id=1, source_target_pairs={{0,16},{16,0},{1,17},{17,1},{2,18},{18,2},{3,19},{19,3},{4,20},{20... | collective-permute-start | bytes 2371592 | tf_op jit(solution)/shard_map/ppermute | solution.py:52
  99.2 2.8 %copy-start = (f32[12352,128]{1,0:T(8,128)S(1)}, f32[12352,128]{1,0:T(8,128)}, u32[]{:S(2)}) copy-start(f32[12352,128]{1,0:T(8,128)} %all-gather.3.cloned.1.call-done) | copy-start | bytes 18972676
  110.0 19.4 %collective-permute-start.20 = (f32[12,128,128]{2,1,0:T(8,128)}, f32[12,128,128]{2,1,0:T(8,128)}, u32[]{:S(2)}, u32[]{:S(2)}) collective-permute-start(f32[12,128,128]{2,1,0:T(8,128)} %shard_map.42), channel_id=1, source_target_pairs={{0,8},{16,24},{1,9},{17,25},{2,10},{18,26},{3,11},{19,27},{4,12},{... | collective-permute-start | bytes 2359304 | tf_op jit(solution)/shard_map/ppermute | solution.py:52
  110.4 2.8 %copy-start.1 = (f32[12352,128]{1,0:T(8,128)S(1)}, f32[12352,128]{1,0:T(8,128)}, u32[]{:S(2)}) copy-start(f32[12352,128]{1,0:T(8,128)} %all-gather.3.cloned.1.call-done) | copy-start | bytes 18972676
  113.2 1.1 copy-start.3
  114.3 1.1 copy-start.5
  115.5 15.1 %copy-start.6 = (f32[6,2,128,128]{3,2,1,0:T(8,128)S(1)}, f32[6,2,128,128]{3,2,1,0:T(8,128)}, u32[]{:S(2)}) copy-start(f32[6,2,128,128]{3,2,1,0:T(8,128)} %param.2) | copy-start | bytes 2359300
  130.6 1.2 copy-start.7
Sparse Core Ops, SparseCore 0:
  10.3 78.5 all-gather.2

commit v2 on v1

v2 whole, which is shorter than its diff:
```python
import functools

import jax
import jax.numpy as jnp
from jax import lax
from jax.experimental import pallas as pl
from jax.experimental.pallas import tpu as pltpu
from jax.sharding import PartitionSpec as P

AXES = ("row", "col")
BS = 128
ROWS = 6
BLOCKS = 12
HALF = BLOCKS // 2 * BS
IDS = 8
PACKED = 2 * HALF + IDS
PIECE = HALF + IDS
UNROLL = 4


def device_id(x, y, z, c):
    return ((x * 2 + y // 2) * 2 + c) * 16 + (y % 2) * 8 + z


def table(move, keep=lambda x, y, z, c: True):
    pairs = []
    for x in range(4):
        for y in range(4):
            for z in range(8):
                for c in range(2):
                    if keep(x, y, z, c):
                        tx, ty, tz, tc = move(x, y, z, c)
                        pairs.append((device_id(x, y, z, c), device_id(tx % 4, ty % 4, tz % 8, tc)))
    return pairs


def near(x, y, z, c):
    return x // 2 == y % 2


IN_PAIR = table(lambda x, y, z, c: (x ^ 1, y, z, c))
CROSS = table(lambda x, y, z, c: (3 - x, y, z, c))
CROSS_NEAR = table(lambda x, y, z, c: (3 - x, y, z, c), near)
Y_FAR_NEAR = table(lambda x, y, z, c: (x, y + 2, z, c), near)
Y_UP = table(lambda x, y, z, c: (x, y + 1, z, c))
Y_DOWN = table(lambda x, y, z, c: (x, y - 1, z, c))
Y_LO = table(lambda x, y, z, c: (x, y ^ 1, z, c))
Z_SPLIT = table(lambda x, y, z, c: (x, y, z + 1 - 2 * c, c))
X_SPLIT = table(lambda x, y, z, c: (x ^ 1 if c else 3 - x, y, z, c))
CORE = table(lambda x, y, z, c: (x, y, z, 1 - c))
Z_UP = table(lambda x, y, z, c: (x, y, z + 1, c))
Z_DOWN = table(lambda x, y, z, c: (x, y, z - 1, c))


def send(value, pairs):
    return lax.ppermute(value, AXES, pairs)


def place():
    row, col = lax.axis_index("row"), lax.axis_index("col")
    return row // 4, (row // 2) % 2, row % 2, col // 8, col % 8


DISTANCES = (0, -1, 1, -2, 2, -3, 3)


def kernel(own_columns, last, started, *refs):
    distances = (() if last == "only" else DISTANCES) + (() if last == "without" else (4,))
    n_left = len(distances)
    lefts, refs = refs[:n_left], refs[n_left:]
    n_right = 9 if own_columns else 8
    rights, out_ids, refs = refs[:n_right], refs[n_right], refs[n_right + 1:]
    if started:
        start, refs = refs[0], refs[1:]
    out, lbuf, rbuf, acc, ids_l, ids_r, ids_o, list_l, list_r, list_o, sem, isem = refs
    zero_row = (1 if last == "only" else 8) * PACKED

    x, y_hi, core, y_lo, z = place()
    near_x = (x // 2) == y_lo
    flip = lax.rem(jnp.where(near_x, x, 3 - x), 2) * 4
    if own_columns:
        y_his = (y_hi, 1 - y_hi)
    else:
        y = y_hi * 2 + y_lo
        y_his = (lax.rem(y + 3, 4) // 2, lax.rem(y + 1, 4) // 2)

    def right_slot(n):
        other, chunk, which = n // 4, (n // 2) % 2, n % 2
        return chunk * 4 + y_his[which] * 2 + (1 - core if other else core)

    def right_copies(n, s):
        at = pl.multiple_of(s * PACKED, 8)
        id_copy = pltpu.make_async_copy(rights[n].at[pl.ds(HALF, IDS), :], ids_r.at[s], isem)
        if own_columns and n == 7:
            return (
                id_copy,
                pltpu.make_async_copy(rights[7].at[:, :], rbuf.at[pl.ds(at, PIECE), :], sem),
                pltpu.make_async_copy(rights[8].at[:, :], rbuf.at[pl.ds(at + PIECE, HALF), :], sem),
            )
        return id_copy, pltpu.make_async_copy(rights[n].at[:, :], rbuf.at[pl.ds(at, PACKED), :], sem)

    blocks_l = [lax.rem(z + distance + 8, 8) for distance in distances]
    slots_l = [block ^ flip for block in blocks_l]
    copies = [pltpu.make_async_copy(out_ids.at[:, :], ids_o, isem)]
    for n, distance in enumerate(distances):
        copies.append(pltpu.make_async_copy(lefts[n].at[pl.ds(HALF, IDS), :], ids_l.at[n], isem))
        at = n * PACKED
        copies.append(pltpu.make_async_copy(lefts[n].at[:, :], lbuf.at[pl.ds(at, PACKED), :], sem))
    if last != "only":
        for n in range(8):
            copies.extend(right_copies(n, right_slot(n)))
    for copy in copies:
        copy.start()
    if last == "only":
        for n in range(8):

            @pl.when(right_slot(n) == slots_l[0])
            def _(n=n):
                for copy in right_copies(n, 0):
                    copy.start()

        copies.extend(right_copies(0, 0))
        slots_r = [0]
    else:
        slots_r = slots_l

    rbuf[pl.ds(zero_row, BS), :] = jnp.zeros((BS, BS), jnp.float32)
    if started:
        acc[:BLOCKS] = start[...]
        acc[BLOCKS] = jnp.zeros((BS, BS), jnp.float32)
    else:
        acc[...] = jnp.zeros_like(acc)
    id_bytes = [copy for copy in copies if copy.dst_sem is isem]
    data_bytes = [copy for copy in copies if copy.dst_sem is sem]
    for copy in id_bytes:
        copy.wait()

    def list_output(o, n):
        i = o // 2
        skip = jnp.where(i >= 3, IDS, 0)
        j = ids_o[0, o]
        for m, block in enumerate(blocks_l):
            first_k = (y_lo * 8 + block) * ROWS
            for t in range(2):
                k = ids_l[m, 0, i * 2 + t].astype(jnp.int32) - first_k
                m1 = (ids_r[slots_r[m], 0, 2 * k + 1] == j).astype(jnp.int32)
                m0 = (ids_r[slots_r[m], 0, 2 * k] == j).astype(jnp.int32)
                list_l[n] = m * PACKED + t * BS + i * 2 * BS + skip
                list_r[n] = slots_r[m] * PACKED + (2 * k + m1) * BS + jnp.where(k >= 3, IDS, 0)
                list_o[n // 2] = o
                n = n + m0 + m1
        list_l[n] = 0
        list_r[n] = zero_row
        return n + n % 2

    n = lax.fori_loop(0, BLOCKS, list_output, 0)
    pairs = n // 2
    for u in range(UNROLL):
        list_o[pairs + u] = BLOCKS
        for e in range(2):
            list_l[n + 2 * u + e] = 0
            list_r[n + 2 * u + e] = zero_row
    for copy in data_bytes:
        copy.wait()

    def split(a):
        hi = a.astype(jnp.bfloat16)
        return hi, (a - hi.astype(jnp.float32)).astype(jnp.bfloat16)

    def left_block(e):
        return lbuf[pl.ds(pl.multiple_of(list_l[e], 8), BS), :]

    def right_block(e):
        return rbuf[pl.ds(pl.multiple_of(list_r[e], 8), BS), :]

    def step(s, carry):
        results = []
        for u in range(UNROLL):
            e = 2 * (s * UNROLL + u)
            a_hi, a_lo = split(jnp.concatenate([left_block(e), left_block(e + 1)], axis=1))
            b_hi, b_lo = split(jnp.concatenate([right_block(e), right_block(e + 1)], axis=0))
            a = jnp.concatenate([a_hi, a_lo], axis=0)
            b = jnp.concatenate([b_hi, b_lo], axis=1)
            r = jnp.dot(a, b, preferred_element_type=jnp.float32)
            results.append(r[:BS, :BS] + (r[:BS, BS:] + r[BS:, :BS]) + r[BS:, BS:])
        for u in range(UNROLL):
            o = list_o[s * UNROLL + u]
            acc[o] = acc[o] + results[u]
        return carry

    lax.fori_loop(0, (pairs + UNROLL - 1) // UNROLL, step, 0)
    out[...] = acc[:BLOCKS]


def contract(own_columns, last, lefts, rights, out_ids, start=None):
    n = {"with": 8, "without": 7, "only": 1}[last]
    longest = 12 * n * 2 + 2 * UNROLL + 2
    started = () if start is None else (start,)
    vmem = pl.BlockSpec(memory_space=pltpu.VMEM)
    return pl.pallas_call(
        functools.partial(kernel, own_columns, last, start is not None),
        out_shape=jax.ShapeDtypeStruct((BLOCKS, BS, BS), jnp.float32),
        in_specs=[pl.BlockSpec(memory_space=pl.ANY)] * (len(lefts) + len(rights) + 1) + [vmem] * len(started),
        out_specs=vmem,
        scratch_shapes=[
            pltpu.VMEM((n * PACKED, BS), jnp.float32),
            pltpu.VMEM(((1 if n == 1 else 8) * PACKED + BS, BS), jnp.float32),
            pltpu.VMEM((BLOCKS + 1, BS, BS), jnp.float32),
            pltpu.SMEM((n, IDS, BS), jnp.float32),
            pltpu.SMEM((1 if n == 1 else 8, IDS, BS), jnp.float32),
            pltpu.SMEM((IDS, BS), jnp.float32),
            pltpu.SMEM((longest,), jnp.int32),
            pltpu.SMEM((longest,), jnp.int32),
            pltpu.SMEM((longest // 2 + 1,), jnp.int32),
            pltpu.SemaphoreType.DMA,
            pltpu.SemaphoreType.DMA,
        ],
        compiler_params=pltpu.CompilerParams(vmem_limit_bytes=(8 if n == 1 else 30) * 2 ** 20),
        cost_estimate=pl.CostEstimate(flops=10 ** 6, bytes_accessed=10 ** 6, transcendentals=0),
    )(*lefts, *rights, out_ids, *started)


STRIPS = 4


def combine_kernel(mine, received, iterate, square, update, s_buf, u_buf, sems):
    copies = []
    for n in range(STRIPS):
        part = pl.ds(n * BLOCKS // STRIPS, BLOCKS // STRIPS)
        total = mine[part] + received[part]
        s_buf[part] = total
        u_buf[part] = 1.5 * iterate[part] - 0.5 * total
        for m, (buf, ref) in enumerate(((s_buf, square), (u_buf, update))):
            copies.append(pltpu.make_async_copy(buf.at[part], ref.at[part], sems.at[n, m]))
            copies[-1].start()
    for copy in copies:
        copy.wait()


def combine(mine, received, iterate):
    shape = jax.ShapeDtypeStruct((BLOCKS, BS, BS), jnp.float32)
    return pl.pallas_call(
        combine_kernel,
        out_shape=(shape, shape),
        in_specs=[pl.BlockSpec(memory_space=pltpu.VMEM)] * 3,
        out_specs=(pl.BlockSpec(memory_space=pl.ANY),) * 2,
        scratch_shapes=[
            pltpu.VMEM((BLOCKS, BS, BS), jnp.float32),
            pltpu.VMEM((BLOCKS, BS, BS), jnp.float32),
            pltpu.SemaphoreType.DMA((STRIPS, 2)),
        ],
        compiler_params=pltpu.CompilerParams(vmem_limit_bytes=8 * 2 ** 20),
    )(mine, received, iterate)


def body(iterate, kept_cols):
    x, y_hi, core, y_lo, z = place()
    is_near = (x // 2) == y_lo

    blocks = iterate.reshape(2 * HALF, BS)
    ids = jnp.pad(kept_cols.reshape(1, BLOCKS).astype(jnp.float32), ((0, IDS - 1), (0, BS - BLOCKS)))
    own = jnp.concatenate([blocks[:HALF], ids, blocks[HALF:]], axis=0)

    partner_ids = send(ids, Y_LO)
    up, down = own, own
    lefts = [own]
    for _ in range(3):
        up, down = send(up, Z_UP), send(down, Z_DOWN)
        lefts += [up, down]
    ends = [send(jnp.where(core == 0, up, down), Z_SPLIT)]

    mine, partner_ids = lax.optimization_barrier((own, partner_ids))
    in_pair, cross = send(mine, IN_PAIR), send(mine, CROSS)
    far = send(mine, Y_FAR_NEAR)
    next1 = jnp.where(is_near, cross, own)
    up1, down1 = send(next1, Y_UP), send(next1, Y_DOWN)
    in_pair, far = lax.optimization_barrier((in_pair, far))
    diagonal = send(jnp.where(core == 0, in_pair, cross), X_SPLIT)
    next2 = jnp.where(is_near, diagonal, in_pair)
    far, next2 = lax.optimization_barrier((far, next2))
    far_cross = send(far, CROSS_NEAR)
    up2, down2 = send(next2, Y_UP), send(next2, Y_DOWN)
    far1 = jnp.where(is_near, far, far_cross)
    far2 = send(far1, IN_PAIR)
    here1 = jnp.where(is_near, own, cross)
    here2 = jnp.where(is_near, in_pair, diagonal)

    swapped1 = [send(v, CORE) for v in (up1, down1)]
    up2, down2, far1, *lefts = lax.optimization_barrier((up2, down2, far1, *lefts))
    rights = [up1, down1, up2, down2] + swapped1 + [send(v, CORE) for v in (up2, down2)]
    partial = contract(False, "without", lefts, rights, partner_ids)
    here1, here2, far1, _ = lax.optimization_barrier((here1, here2, far1, up2))
    others = [send(v, CORE) for v in (here1, far1, here2)]
    partial, *others = lax.optimization_barrier((partial, *others))
    partial = contract(False, "only", ends, rights, partner_ids, partial)
    received = send(partial, Y_LO)

    far2, _ = lax.optimization_barrier((far2, partial))
    others += [send(far2[:PIECE], CORE), send(far2[PIECE:], CORE)]
    mine = contract(True, "with", lefts + ends, [here1, far1, here2, far2] + others, ids)

    square, update = combine(mine, received, iterate.reshape(BLOCKS, BS, BS))
    return (square.reshape(iterate.shape), update.reshape(iterate.shape))


def solution(mesh):
    in_specs = (P("row", "col", None, None), P("row", "col"))
    out_specs = (P("row", "col", None, None), P("row", "col", None, None))
    return jax.shard_map(body, mesh=mesh, in_specs=in_specs, out_specs=out_specs, check_vma=False)
```

time: 140 us -> 113 us (0.81); the launches traced: 139 us -> 113 us
  local copies, waits for them, and re-layouts: 18.9 us -> 1.41 us
  between operations: 14.3 us -> 0.98 us
  Pallas kernels: 15.2 us -> 20.7 us
  starting transfers between devices: 40.3 us -> 44.8 us
  other arithmetic: 7.73 us -> 4.67 us
  waiting for transfers between devices: 42.1 us -> 40.4 us
    unnamed x17 -> x2, local copies, waits for them, and re-layouts: 8.01 us -> 0.01 us
    slice x21 -> x3, local copies, waits for them, and re-layouts: 8.95 us -> 1.22 us  [the longest x1 1.17 us: body(): own = jnp.concatenate([blocks[:HALF], ids, blocks[HALF:]], axis=0)]
    pallas_call x2 -> x4, Pallas kernels: 15.2 us -> 20.7 us  [the longest x3 19.5 us: contract(): pl.pallas_call(functools.partial(kernel, own_columns, last, start is not...]
    ppermute x21 -> x28, starting transfers between devices: 40.3 us -> 44.8 us  [send(): return lax.ppermute(value, AXES, pairs)]
    concatenate x1, other arithmetic: 2.08 us -> 0.05 us  [body(): own = jnp.concatenate([blocks[:HALF], ids, blocks[HALF:]], axis=0)]
    ppermute x21 -> x28, waiting for transfers between devices: 42 us -> 40.4 us  [send(): return lax.ppermute(value, AXES, pairs)]
  transfers between devices with their start and end apart: 22 -> 28, of which waited for: 7 -> 10; matrix products, arithmetic and copies ran while one was open for 9% -> 5% of each run, Pallas kernels for 5% -> 17%
where the time goes in v2:
time: 113 us
  starting transfers between devices  44.8 us (40%)
  waiting for transfers between devices  40.4 us (36%)
  Pallas kernels  20.7 us (18%)
  other arithmetic  4.67 us (4%)
  local copies, waits for them, and re-layouts  1.41 us (1%)
    ppermute x28, starting transfers between devices, send(): return lax.ppermute(value, AXES, pairs)  44.8 us
    ppermute x28, waiting for transfers between devices, send(): return lax.ppermute(value, AXES, pairs)  40.4 us
    pallas_call x3, Pallas kernels, contract(): pl.pallas_call(functools.partial(kernel, own_columns, last, start is not...  19.5 us
  transfers between devices with their start and end apart: 28, of which 10 were waited for; matrix products, arithmetic and copies ran while one was open for 5% of the time, Pallas kernels for 17%

profile of v2, /device:TPU:1, one launch (start us, length us, event | category | flops | bytes accessed | tf_op | source)
XLA Modules:
  0.0 113.0 jit_solution(3048115277655607920)
XLA Ops:
  0.6 0.7 convert_element_type.16
  1.5 2.2 %collective-permute-start = (f32[8,128]{1,0:T(8,128)S(1)}, f32[8,128]{1,0:T(8,128)S(1)}, u32[]{:S(2)}, u32[]{:S(2)}) collective-permute-start(f32[8,128]{1,0:T(8,128)S(1)} %pad.4.refs_17_), channel_id=1, source_target_pairs={{0,8},{16,24},{1,9},{17,25},{2,10},{18,26},{3,11},{19,27},{4,12},{... | collective-permute-start | bytes 12296 | tf_op jit(solution)/shard_map/ppermute | solution.py:56
  3.7 1.2 %fusion = (f32[3,2,128,128]{3,2,1,0:T(8,128)S(1)}, f32[3,2,128,128]{3,2,1,0:T(8,128)S(1)}) fusion(f32[6,2,128,128]{3,2,1,0:T(8,128)} %param.2), kind=kLoop, calls=%fused_computation.8 | loop fusion | bytes 1572864 | tf_op jit(solution)/shard_map/slice | solution.py:262
  4.9 1.7 %collective-permute-start.8 = (f32[1544,128]{1,0:T(8,128)S(1)}, f32[1544,128]{1,0:T(8,128)S(1)}, u32[]{:S(2)}, u32[]{:S(2)}) collective-permute-start(f32[1544,128]{1,0:T(8,128)S(1)} %pad_maximum_fusion.refs_0_), channel_id=1, source_target_pairs={{0,1},{16,17},{1,2},{17,18},{2,3},{18,19},{3,4},{19,20},{4,5},{20,... | collective-permute-start | bytes 2371592 | tf_op jit(solution)/shard_map/ppermute | solution.py:56
  6.7 1.2 %collective-permute-start.1 = (f32[1544,128]{1,0:T(8,128)S(1)}, f32[1544,128]{1,0:T(8,128)}, u32[]{:S(2)}, u32[]{:S(2)}) collective-permute-start(f32[1544,128]{1,0:T(8,128)S(1)} %pad_maximum_fusion.refs_0_), channel_id=1, source_target_pairs={{0,64},{16,80},{1,65},{17,81},{2,66},{18,82},{3,67},{19,83},{4,68}... | collective-permute-start | bytes 2371592 | tf_op jit(solution)/shard_map/ppermute | solution.py:56
  7.9 4.5 %collective-permute-start.2 = (f32[1544,128]{1,0:T(8,128)S(1)}, f32[1544,128]{1,0:T(8,128)}, u32[]{:S(2)}, u32[]{:S(2)}) collective-permute-start(f32[1544,128]{1,0:T(8,128)S(1)} %pad_maximum_fusion.refs_0_), channel_id=1, source_target_pairs={{0,32},{16,48},{1,33},{17,49},{2,34},{18,50},{3,35},{19,51},{4,36}... | collective-permute-start | bytes 2371592 | tf_op jit(solution)/shard_map/ppermute | solution.py:56
  12.5 4.2 %collective-permute-start.9 = (f32[1544,128]{1,0:T(8,128)S(1)}, f32[1544,128]{1,0:T(8,128)S(1)}, u32[]{:S(2)}, u32[]{:S(2)}) collective-permute-start(f32[1544,128]{1,0:T(8,128)S(1)} %pad_maximum_fusion.refs_0_), channel_id=1, source_target_pairs={{0,7},{16,23},{1,0},{17,16},{2,1},{18,17},{3,2},{19,18},{4,3},{20,... | collective-permute-start | bytes 2371592 | tf_op jit(solution)/shard_map/ppermute | solution.py:56
  16.7 11.1 %collective-permute-done.8.refs_1_ = f32[1544,128]{1,0:T(8,128)S(1)} collective-permute-done((f32[1544,128]{1,0:T(8,128)S(1)}, f32[1544,128]{1,0:T(8,128)S(1)}, u32[]{:S(2)}, u32[]{:S(2)}) %collective-permute-start.8) | collective-permute-done | bytes 790560 | tf_op jit(solution)/shard_map/ppermute | solution.py:56
  27.7 1.2 %collective-permute-done.2 = f32[1544,128]{1,0:T(8,128)} collective-permute-done((f32[1544,128]{1,0:T(8,128)S(1)}, f32[1544,128]{1,0:T(8,128)}, u32[]{:S(2)}, u32[]{:S(2)}) %collective-permute-start.2) | collective-permute-done | bytes 790560 | tf_op jit(solution)/shard_map/ppermute | solution.py:56
  29.0 2.2 %collective-permute-done.3 = f32[1544,128]{1,0:T(8,128)} collective-permute-done((f32[1544,128]{1,0:T(8,128)S(1)}, f32[1544,128]{1,0:T(8,128)}, u32[]{:S(2)}, u32[]{:S(2)}) %collective-permute-start.3) | collective-permute-done | bytes 790560 | tf_op jit(solution)/shard_map/ppermute | solution.py:56
  31.1 1.4 %broadcast_select_fusion.2 = (f32[1544,128]{1,0:T(8,128)S(1)}, f32[1544,128]{1,0:T(8,128)S(1)}, f32[1544,128]{1,0:T(8,128)S(1)}) fusion(f32[1544,128]{1,0:T(8,128)} %collective-permute-done.3, pred[]{:T(512)S(6)} %eq.9, f32[768,128]{1,0:T(8,128)S(1)} %bitcast.9, f32[8,128]{1,0:T(8,128)S(1)} %pad.4.refs_17_, f32[768,128]{1,0:T(8,128)S(1)} %bitcast.7, ...), kind=kLoop, calls=%fused_computation.3 | loop fusion | flops 988160 | bytes 4743170 | tf_op jit(solution)/shard_map/jit(_where)/select_n | solution.py:275
  32.6 3.6 %collective-permute-start.11 = (f32[1544,128]{1,0:T(8,128)S(1)}, f32[1544,128]{1,0:T(8,128)S(1)}, u32[]{:S(2)}, u32[]{:S(2)}) collective-permute-start(f32[1544,128]{1,0:T(8,128)S(1)} %collective-permute-done.9.refs_2_), channel_id=1, source_target_pairs={{0,7},{16,23},{1,0},{17,16},{2,1},{18,17},{3,2},{19,18},{4,3},{20,... | collective-permute-start | bytes 2371592 | tf_op jit(solution)/shard_map/ppermute | solution.py:56
  36.5 2.3 %collective-permute-start.17 = (f32[1544,128]{1,0:T(8,128)S(1)}, f32[1544,128]{1,0:T(8,128)S(1)}, u32[]{:S(2)}, u32[]{:S(2)}) collective-permute-start(f32[1544,128]{1,0:T(8,128)S(1)} %get-tuple-element.54), channel_id=1, source_target_pairs={{0,40},{16,56},{1,41},{17,57},{2,42},{18,58},{3,43},{19,59},{4,44}... | collective-permute-start | bytes 2371592 | tf_op jit(solution)/shard_map/ppermute | solution.py:56
  38.8 7.8 %collective-permute-done.10.refs_3_ = f32[1544,128]{1,0:T(8,128)S(1)} collective-permute-done((f32[1544,128]{1,0:T(8,128)S(1)}, f32[1544,128]{1,0:T(8,128)S(1)}, u32[]{:S(2)}, u32[]{:S(2)}) %collective-permute-start.10) | collective-permute-done | bytes 790560 | tf_op jit(solution)/shard_map/ppermute | solution.py:56
  46.6 1.2 %broadcast_select_fusion.3 = (f32[1544,128]{1,0:T(8,128)S(1)}, f32[1544,128]{1,0:T(8,128)S(1)}) fusion(f32[1544,128]{1,0:T(8,128)} %collective-permute-done.1, f32[1544,128]{1,0:T(8,128)S(1)} %collective-permute-done.4, pred[]{:T(512)S(6)} %eq.9), kind=kLoop, calls=%fused_computation.4 | loop fusion | flops 395264 | bytes 3162113 | tf_op jit(solution)/shard_map/jit(_where)/select_n | solution.py:286
  47.9 4.4 %collective-permute-start.7 = (f32[1544,128]{1,0:T(8,128)}, f32[1544,128]{1,0:T(8,128)S(1)}, u32[]{:S(2)}, u32[]{:S(2)}) collective-permute-start(f32[1544,128]{1,0:T(8,128)} %collective-permute-done.2), channel_id=1, source_target_pairs={{0,192},{16,208},{1,193},{17,209},{2,194},{18,210},{3,195},{19,211... | collective-permute-start | bytes 2371592 | tf_op jit(solution)/shard_map/ppermute | solution.py:56
  52.3 2.7 %collective-permute-start.13 = (f32[1544,128]{1,0:T(8,128)S(1)}, f32[1544,128]{1,0:T(8,128)S(1)}, u32[]{:S(2)}, u32[]{:S(2)}) collective-permute-start(f32[1544,128]{1,0:T(8,128)S(1)} %collective-permute-done.11.refs_4_), channel_id=1, source_target_pairs={{0,7},{16,23},{1,0},{17,16},{2,1},{18,17},{3,2},{19,18},{4,3},{20,... | collective-permute-start | bytes 2371592 | tf_op jit(solution)/shard_map/ppermute | solution.py:56
  55.1 2.7 %collective-permute-start.6 = (f32[1544,128]{1,0:T(8,128)S(1)}, f32[1544,128]{1,0:T(8,128)S(1)}, u32[]{:S(2)}, u32[]{:S(2)}) collective-permute-start(f32[1544,128]{1,0:T(8,128)S(1)} %get-tuple-element.31), channel_id=1, source_target_pairs={{0,40},{16,56},{1,41},{17,57},{2,42},{18,58},{3,43},{19,59},{4,44}... | collective-permute-start | bytes 2371592 | tf_op jit(solution)/shard_map/ppermute | solution.py:56
  57.8 6.8 %collective-permute-done.12.refs_5_ = f32[1544,128]{1,0:T(8,128)S(1)} collective-permute-done((f32[1544,128]{1,0:T(8,128)S(1)}, f32[1544,128]{1,0:T(8,128)S(1)}, u32[]{:S(2)}, u32[]{:S(2)}) %collective-permute-start.12) | collective-permute-done | bytes 790560 | tf_op jit(solution)/shard_map/ppermute | solution.py:56
  64.6 3.3 %collective-permute-start.18 = (f32[1544,128]{1,0:T(8,128)S(1)}, f32[1544,128]{1,0:T(8,128)S(1)}, u32[]{:S(2)}, u32[]{:S(2)}) collective-permute-start(f32[1544,128]{1,0:T(8,128)S(1)} %collective-permute-done.16.refs_7_.refs_1_), channel_id=1, source_target_pairs={{0,16},{16,0},{1,17},{17,1},{2,18},{18,2},{3,19},{19,3},{4,20},{20... | collective-permute-start | bytes 2371592 | tf_op jit(solution)/shard_map/ppermute | solution.py:56
  67.9 2.5 %collective-permute-start.19 = (f32[1544,128]{1,0:T(8,128)S(1)}, f32[1544,128]{1,0:T(8,128)S(1)}, u32[]{:S(2)}, u32[]{:S(2)}) collective-permute-start(f32[1544,128]{1,0:T(8,128)S(1)} %collective-permute-done.17.refs_8_.refs_2_), channel_id=1, source_target_pairs={{0,16},{16,0},{1,17},{17,1},{2,18},{18,2},{3,19},{19,3},{4,20},{20... | collective-permute-start | bytes 2371592 | tf_op jit(solution)/shard_map/ppermute | solution.py:56
  70.4 1.2 %broadcast_select_fusion.5.refs_9_ = f32[1544,128]{1,0:T(8,128)S(1)} fusion(f32[1544,128]{1,0:T(8,128)} %collective-permute-done.2, f32[1544,128]{1,0:T(8,128)S(1)} %collective-permute-done.7, pred[]{:T(512)S(6)} %eq.9), kind=kLoop, calls=%fused_computation.6 | loop fusion | flops 197632 | bytes 2371585 | tf_op jit(solution)/shard_map/jit(_where)/select_n | solution.py:283
  72.2 4.1 %collective-permute-start.20 = (f32[1544,128]{1,0:T(8,128)S(1)}, f32[1544,128]{1,0:T(8,128)S(1)}, u32[]{:S(2)}, u32[]{:S(2)}) collective-permute-start(f32[1544,128]{1,0:T(8,128)S(1)} %collective-permute-done.5.refs_9_.refs_3_), channel_id=1, source_target_pairs={{0,16},{16,0},{1,17},{17,1},{2,18},{18,2},{3,19},{19,3},{4,20},{20... | collective-permute-start | bytes 2371592 | tf_op jit(solution)/shard_map/ppermute | solution.py:56
  77.5 0.8 collective-permute-done.20.refs_13_.refs_7_
  78.4 1.0 collective-permute-done.21.refs_14_.refs_8_
  79.4 2.5 %collective-permute-start.15 = (f32[1544,128]{1,0:T(8,128)S(1)}, f32[1544,128]{1,0:T(8,128)S(1)}, u32[]{:S(2)}, u32[]{:S(2)}) collective-permute-start(f32[1544,128]{1,0:T(8,128)S(1)} %broadcast_select_fusion.5.refs_9_), channel_id=1, source_target_pairs={{0,64},{16,80},{1,65},{17,81},{2,66},{18,82},{3,67},{19,83},{4,68}... | collective-permute-start | bytes 2371592 | tf_op jit(solution)/shard_map/ppermute | solution.py:56
  81.9 8.2 %shard_map.41.refs_10_ = f32[12,128,128]{2,1,0:T(8,128)S(1)} custom-call(f32[1544,128]{1,0:T(8,128)S(1)} %pad_maximum_fusion.refs_0_, f32[1544,128]{1,0:T(8,128)S(1)} %collective-permute-done.8.refs_1_, f32[1544,128]{1,0:T(8,128)S(1)} %collective-permute-done.9.refs_2_, f32[1544,128]{1,0:T(8,128)S(1)} %collective-permute-done.10.refs_3_, ...), custom_call_target="tpu_custom_call" | custom-call | flops 1000000 | bytes 1000000 | tf_op jit(solution)/shard_map/pallas_call | solution.py:200
  90.1 2.0 %shard_map.42 = f32[12,128,128]{2,1,0:T(8,128)S(1)} custom-call(f32[1544,128]{1,0:T(8,128)S(1)} %collective-permute-done.14.refs_0_.refs_7_, f32[1544,128]{1,0:T(8,128)S(1)} %collective-permute-done.16.refs_7_.refs_1_, f32[1544,128]{1,0:T(8,128)S(1)} %collective-permute-done.17.refs_8_.refs_2_, f32[1544,128]{1,0:T(8,128)S(1)} %collective-permute-done.5.refs_9_.refs_3_, ...), custom_call_target="tpu_custom_call" | custom-call | flops 1000000 | bytes 1000000 | tf_op jit(solution)/shard_map/pallas_call | solution.py:200
  92.6 7.3 %collective-permute-done.15.refs_11_ = f32[1544,128]{1,0:T(8,128)S(1)} collective-permute-done((f32[1544,128]{1,0:T(8,128)S(1)}, f32[1544,128]{1,0:T(8,128)S(1)}, u32[]{:S(2)}, u32[]{:S(2)}) %collective-permute-start.15) | collective-permute-done | bytes 790560 | tf_op jit(solution)/shard_map/ppermute | solution.py:56
  100.6 1.7 %collective-permute-done.26.refs_16_ = f32[768,128]{1,0:T(8,128)S(1)} collective-permute-done((f32[768,128]{1,0:T(8,128)S(1)}, f32[768,128]{1,0:T(8,128)S(1)}, u32[]{:S(2)}, u32[]{:S(2)}) %collective-permute-start.26) | collective-permute-done | bytes 393248 | tf_op jit(solution)/shard_map/ppermute | solution.py:56
  102.3 9.3 %shard_map.43.mine = f32[12,128,128]{2,1,0:T(8,128)S(1)} custom-call(f32[1544,128]{1,0:T(8,128)S(1)} %pad_maximum_fusion.refs_0_, f32[1544,128]{1,0:T(8,128)S(1)} %collective-permute-done.8.refs_1_, f32[1544,128]{1,0:T(8,128)S(1)} %collective-permute-done.9.refs_2_, f32[1544,128]{1,0:T(8,128)S(1)} %collective-permute-done.10.refs_3_, ...), custom_call_target="tpu_custom_call" | custom-call | flops 1000000 | bytes 1000000 | tf_op jit(solution)/shard_map/pallas_call | solution.py:200
  111.6 1.2 %shard_map.44 = (f32[12,128,128]{2,1,0:T(8,128)}, f32[12,128,128]{2,1,0:T(8,128)}) custom-call(f32[12,128,128]{2,1,0:T(8,128)S(1)} %shard_map.43.mine, f32[12,128,128]{2,1,0:T(8,128)S(1)} %collective-permute-done.27.received, f32[12,128,128]{2,1,0:T(8,128)S(1)} %bitcast.5), custom_call_target="tpu_custom_call" | custom-call | tf_op jit(solution)/shard_map/pallas_call | solution.py:242
  (42 shorter events, 3.9 us)
Async XLA Ops:
  1.5 5.2 %collective-permute-start = (f32[8,128]{1,0:T(8,128)S(1)}, f32[8,128]{1,0:T(8,128)S(1)}, u32[]{:S(2)}, u32[]{:S(2)}) collective-permute-start(f32[8,128]{1,0:T(8,128)S(1)} %pad.4.refs_17_), channel_id=1, source_target_pairs={{0,8},{16,24},{1,9},{17,25},{2,10},{18,26},{3,11},{19,27},{4,12},{... | collective-permute-start | bytes 12296 | tf_op jit(solution)/shard_map/ppermute | solution.py:56
  4.9 22.8 %collective-permute-start.8 = (f32[1544,128]{1,0:T(8,128)S(1)}, f32[1544,128]{1,0:T(8,128)S(1)}, u32[]{:S(2)}, u32[]{:S(2)}) collective-permute-start(f32[1544,128]{1,0:T(8,128)S(1)} %pad_maximum_fusion.refs_0_), channel_id=1, source_target_pairs={{0,1},{16,17},{1,2},{17,18},{2,3},{18,19},{3,4},{19,20},{4,5},{20,... | collective-permute-start | bytes 2371592 | tf_op jit(solution)/shard_map/ppermute | solution.py:56
  6.7 21.1 %collective-permute-start.1 = (f32[1544,128]{1,0:T(8,128)S(1)}, f32[1544,128]{1,0:T(8,128)}, u32[]{:S(2)}, u32[]{:S(2)}) collective-permute-start(f32[1544,128]{1,0:T(8,128)S(1)} %pad_maximum_fusion.refs_0_), channel_id=1, source_target_pairs={{0,64},{16,80},{1,65},{17,81},{2,66},{18,82},{3,67},{19,83},{4,68}... | collective-permute-start | bytes 2371592 | tf_op jit(solution)/shard_map/ppermute | solution.py:56
  7.9 21.1 %collective-permute-start.2 = (f32[1544,128]{1,0:T(8,128)S(1)}, f32[1544,128]{1,0:T(8,128)}, u32[]{:S(2)}, u32[]{:S(2)}) collective-permute-start(f32[1544,128]{1,0:T(8,128)S(1)} %pad_maximum_fusion.refs_0_), channel_id=1, source_target_pairs={{0,32},{16,48},{1,33},{17,49},{2,34},{18,50},{3,35},{19,51},{4,36}... | collective-permute-start | bytes 2371592 | tf_op jit(solution)/shard_map/ppermute | solution.py:56
  12.4 18.7 %collective-permute-start.3 = (f32[1544,128]{1,0:T(8,128)S(1)}, f32[1544,128]{1,0:T(8,128)}, u32[]{:S(2)}, u32[]{:S(2)}) collective-permute-start(f32[1544,128]{1,0:T(8,128)S(1)} %pad_maximum_fusion.refs_0_), channel_id=1, source_target_pairs={{0,192},{16,208},{1,193},{17,209},{2,194},{18,210},{3,195},{19,211... | collective-permute-start | bytes 2371592 | tf_op jit(solution)/shard_map/ppermute | solution.py:56
  12.5 20.1 %collective-permute-start.9 = (f32[1544,128]{1,0:T(8,128)S(1)}, f32[1544,128]{1,0:T(8,128)S(1)}, u32[]{:S(2)}, u32[]{:S(2)}) collective-permute-start(f32[1544,128]{1,0:T(8,128)S(1)} %pad_maximum_fusion.refs_0_), channel_id=1, source_target_pairs={{0,7},{16,23},{1,0},{17,16},{2,1},{18,17},{3,2},{19,18},{4,3},{20,... | collective-permute-start | bytes 2371592 | tf_op jit(solution)/shard_map/ppermute | solution.py:56
  27.7 18.9 %collective-permute-start.10 = (f32[1544,128]{1,0:T(8,128)S(1)}, f32[1544,128]{1,0:T(8,128)S(1)}, u32[]{:S(2)}, u32[]{:S(2)}) collective-permute-start(f32[1544,128]{1,0:T(8,128)S(1)} %collective-permute-done.8.refs_1_), channel_id=1, source_target_pairs={{0,1},{16,17},{1,2},{17,18},{2,3},{18,19},{3,4},{19,20},{4,5},{20,... | collective-permute-start | bytes 2371592 | tf_op jit(solution)/shard_map/ppermute | solution.py:56
  32.5 14.1 %collective-permute-start.4 = (f32[1544,128]{1,0:T(8,128)S(1)}, f32[1544,128]{1,0:T(8,128)S(1)}, u32[]{:S(2)}, u32[]{:S(2)}) collective-permute-start(f32[1544,128]{1,0:T(8,128)S(1)} %get-tuple-element.58), channel_id=1, source_target_pairs={{0,192},{16,80},{1,193},{17,81},{2,194},{18,82},{3,195},{19,83},{4... | collective-permute-start | bytes 2371592 | tf_op jit(solution)/shard_map/ppermute | solution.py:56
  32.6 19.7 %collective-permute-start.11 = (f32[1544,128]{1,0:T(8,128)S(1)}, f32[1544,128]{1,0:T(8,128)S(1)}, u32[]{:S(2)}, u32[]{:S(2)}) collective-permute-start(f32[1544,128]{1,0:T(8,128)S(1)} %collective-permute-done.9.refs_2_), channel_id=1, source_target_pairs={{0,7},{16,23},{1,0},{17,16},{2,1},{18,17},{3,2},{19,18},{4,3},{20,... | collective-permute-start | bytes 2371592 | tf_op jit(solution)/shard_map/ppermute | solution.py:56
  36.2 18.9 %collective-permute-start.16 = (f32[1544,128]{1,0:T(8,128)S(1)}, f32[1544,128]{1,0:T(8,128)S(1)}, u32[]{:S(2)}, u32[]{:S(2)}) collective-permute-start(f32[1544,128]{1,0:T(8,128)S(1)} %get-tuple-element.54), channel_id=1, source_target_pairs={{0,8},{16,24},{1,9},{17,25},{2,10},{18,26},{3,11},{19,27},{4,12},{... | collective-permute-start | bytes 2371592 | tf_op jit(solution)/shard_map/ppermute | solution.py:56
  36.5 18.5 %collective-permute-start.17 = (f32[1544,128]{1,0:T(8,128)S(1)}, f32[1544,128]{1,0:T(8,128)S(1)}, u32[]{:S(2)}, u32[]{:S(2)}) collective-permute-start(f32[1544,128]{1,0:T(8,128)S(1)} %get-tuple-element.54), channel_id=1, source_target_pairs={{0,40},{16,56},{1,41},{17,57},{2,42},{18,58},{3,43},{19,59},{4,44}... | collective-permute-start | bytes 2371592 | tf_op jit(solution)/shard_map/ppermute | solution.py:56
  46.6 18.0 %collective-permute-start.12 = (f32[1544,128]{1,0:T(8,128)S(1)}, f32[1544,128]{1,0:T(8,128)S(1)}, u32[]{:S(2)}, u32[]{:S(2)}) collective-permute-start(f32[1544,128]{1,0:T(8,128)S(1)} %collective-permute-done.10.refs_3_), channel_id=1, source_target_pairs={{0,1},{16,17},{1,2},{17,18},{2,3},{18,19},{3,4},{19,20},{4,5},{20,... | collective-permute-start | bytes 2371592 | tf_op jit(solution)/shard_map/ppermute | solution.py:56
  47.9 20.0 %collective-permute-start.7 = (f32[1544,128]{1,0:T(8,128)}, f32[1544,128]{1,0:T(8,128)S(1)}, u32[]{:S(2)}, u32[]{:S(2)}) collective-permute-start(f32[1544,128]{1,0:T(8,128)} %collective-permute-done.2), channel_id=1, source_target_pairs={{0,192},{16,208},{1,193},{17,209},{2,194},{18,210},{3,195},{19,211... | collective-permute-start | bytes 2371592 | tf_op jit(solution)/shard_map/ppermute | solution.py:56
  52.3 19.3 %collective-permute-start.13 = (f32[1544,128]{1,0:T(8,128)S(1)}, f32[1544,128]{1,0:T(8,128)S(1)}, u32[]{:S(2)}, u32[]{:S(2)}) collective-permute-start(f32[1544,128]{1,0:T(8,128)S(1)} %collective-permute-done.11.refs_4_), channel_id=1, source_target_pairs={{0,7},{16,23},{1,0},{17,16},{2,1},{18,17},{3,2},{19,18},{4,3},{20,... | collective-permute-start | bytes 2371592 | tf_op jit(solution)/shard_map/ppermute | solution.py:56
  55.1 17.1 %collective-permute-start.5 = (f32[1544,128]{1,0:T(8,128)S(1)}, f32[1544,128]{1,0:T(8,128)S(1)}, u32[]{:S(2)}, u32[]{:S(2)}) collective-permute-start(f32[1544,128]{1,0:T(8,128)S(1)} %get-tuple-element.31), channel_id=1, source_target_pairs={{0,8},{16,24},{1,9},{17,25},{2,10},{18,26},{3,11},{19,27},{4,12},{... | collective-permute-start | bytes 2371592 | tf_op jit(solution)/shard_map/ppermute | solution.py:56
  55.1 17.1 %collective-permute-start.6 = (f32[1544,128]{1,0:T(8,128)S(1)}, f32[1544,128]{1,0:T(8,128)S(1)}, u32[]{:S(2)}, u32[]{:S(2)}) collective-permute-start(f32[1544,128]{1,0:T(8,128)S(1)} %get-tuple-element.31), channel_id=1, source_target_pairs={{0,40},{16,56},{1,41},{17,57},{2,42},{18,58},{3,43},{19,59},{4,44}... | collective-permute-start | bytes 2371592 | tf_op jit(solution)/shard_map/ppermute | solution.py:56
  64.6 12.3 %collective-permute-start.18 = (f32[1544,128]{1,0:T(8,128)S(1)}, f32[1544,128]{1,0:T(8,128)S(1)}, u32[]{:S(2)}, u32[]{:S(2)}) collective-permute-start(f32[1544,128]{1,0:T(8,128)S(1)} %collective-permute-done.16.refs_7_.refs_1_), channel_id=1, source_target_pairs={{0,16},{16,0},{1,17},{17,1},{2,18},{18,2},{3,19},{19,3},{4,20},{20... | collective-permute-start | bytes 2371592 | tf_op jit(solution)/shard_map/ppermute | solution.py:56
  67.9 9.0 %collective-permute-start.19 = (f32[1544,128]{1,0:T(8,128)S(1)}, f32[1544,128]{1,0:T(8,128)S(1)}, u32[]{:S(2)}, u32[]{:S(2)}) collective-permute-start(f32[1544,128]{1,0:T(8,128)S(1)} %collective-permute-done.17.refs_8_.refs_2_), channel_id=1, source_target_pairs={{0,16},{16,0},{1,17},{17,1},{2,18},{18,2},{3,19},{19,3},{4,20},{20... | collective-permute-start | bytes 2371592 | tf_op jit(solution)/shard_map/ppermute | solution.py:56
  72.2 6.0 %collective-permute-start.20 = (f32[1544,128]{1,0:T(8,128)S(1)}, f32[1544,128]{1,0:T(8,128)S(1)}, u32[]{:S(2)}, u32[]{:S(2)}) collective-permute-start(f32[1544,128]{1,0:T(8,128)S(1)} %collective-permute-done.5.refs_9_.refs_3_), channel_id=1, source_target_pairs={{0,16},{16,0},{1,17},{17,1},{2,18},{18,2},{3,19},{19,3},{4,20},{20... | collective-permute-start | bytes 2371592 | tf_op jit(solution)/shard_map/ppermute | solution.py:56
  76.3 3.0 %collective-permute-start.21 = (f32[1544,128]{1,0:T(8,128)S(1)}, f32[1544,128]{1,0:T(8,128)S(1)}, u32[]{:S(2)}, u32[]{:S(2)}) collective-permute-start(f32[1544,128]{1,0:T(8,128)S(1)} %collective-permute-done.6.refs_10_.refs_4_), channel_id=1, source_target_pairs={{0,16},{16,0},{1,17},{17,1},{2,18},{18,2},{3,19},{19,3},{4,20},{20... | collective-permute-start | bytes 2371592 | tf_op jit(solution)/shard_map/ppermute | solution.py:56
  76.3 13.7 %collective-permute-start.22 = (f32[1544,128]{1,0:T(8,128)S(1)}, f32[1544,128]{1,0:T(8,128)S(1)}, u32[]{:S(2)}, u32[]{:S(2)}) collective-permute-start(f32[1544,128]{1,0:T(8,128)S(1)} %get-tuple-element.42.refs_8_), channel_id=1, source_target_pairs={{0,16},{16,0},{1,17},{17,1},{2,18},{18,2},{3,19},{19,3},{4,20},{20... | collective-permute-start | bytes 2371592 | tf_op jit(solution)/shard_map/ppermute | solution.py:56
  76.9 13.2 %collective-permute-start.23 = (f32[1544,128]{1,0:T(8,128)S(1)}, f32[1544,128]{1,0:T(8,128)S(1)}, u32[]{:S(2)}, u32[]{:S(2)}) collective-permute-start(f32[1544,128]{1,0:T(8,128)S(1)} %broadcast_select_fusion.5.refs_9_), channel_id=1, source_target_pairs={{0,16},{16,0},{1,17},{17,1},{2,18},{18,2},{3,19},{19,3},{4,20},{20... | collective-permute-start | bytes 2371592 | tf_op jit(solution)/shard_map/ppermute | solution.py:56
  76.9 13.2 %collective-permute-start.24 = (f32[1544,128]{1,0:T(8,128)S(1)}, f32[1544,128]{1,0:T(8,128)S(1)}, u32[]{:S(2)}, u32[]{:S(2)}) collective-permute-start(f32[1544,128]{1,0:T(8,128)S(1)} %get-tuple-element.44.refs_10_), channel_id=1, source_target_pairs={{0,16},{16,0},{1,17},{17,1},{2,18},{18,2},{3,19},{19,3},{4,20},{20... | collective-permute-start | bytes 2371592 | tf_op jit(solution)/shard_map/ppermute | solution.py:56
  78.3 11.8 %collective-permute-start.14 = (f32[1544,128]{1,0:T(8,128)S(1)}, f32[1544,128]{1,0:T(8,128)S(1)}, u32[]{:S(2)}, u32[]{:S(2)}) collective-permute-start(f32[1544,128]{1,0:T(8,128)S(1)} %broadcast_select_fusion), channel_id=1, source_target_pairs={{0,1},{16,23},{1,2},{17,16},{2,3},{18,17},{3,4},{19,18},{4,5},{20,... | collective-permute-start | bytes 2371592 | tf_op jit(solution)/shard_map/ppermute | solution.py:56
  79.4 20.5 %collective-permute-start.15 = (f32[1544,128]{1,0:T(8,128)S(1)}, f32[1544,128]{1,0:T(8,128)S(1)}, u32[]{:S(2)}, u32[]{:S(2)}) collective-permute-start(f32[1544,128]{1,0:T(8,128)S(1)} %broadcast_select_fusion.5.refs_9_), channel_id=1, source_target_pairs={{0,64},{16,80},{1,65},{17,81},{2,66},{18,82},{3,67},{19,83},{4,68}... | collective-permute-start | bytes 2371592 | tf_op jit(solution)/shard_map/ppermute | solution.py:56
  92.1 19.5 %collective-permute-start.27 = (f32[12,128,128]{2,1,0:T(8,128)S(1)}, f32[12,128,128]{2,1,0:T(8,128)S(1)}, u32[]{:S(2)}, u32[]{:S(2)}) collective-permute-start(f32[12,128,128]{2,1,0:T(8,128)S(1)} %shard_map.42), channel_id=1, source_target_pairs={{0,8},{16,24},{1,9},{17,25},{2,10},{18,26},{3,11},{19,27},{4,12},{... | collective-permute-start | bytes 2359304 | tf_op jit(solution)/shard_map/ppermute | solution.py:56
  99.9 2.4 %collective-permute-start.25 = (f32[776,128]{1,0:T(8,128)S(1)}, f32[776,128]{1,0:T(8,128)S(1)}, u32[]{:S(2)}, u32[]{:S(2)}) collective-permute-start(f32[776,128]{1,0:T(8,128)S(1)} %slice.22), channel_id=1, source_target_pairs={{0,16},{16,0},{1,17},{17,1},{2,18},{18,2},{3,19},{19,3},{4,20},{20... | collective-permute-start | bytes 1191944 | tf_op jit(solution)/shard_map/ppermute | solution.py:56
  100.2 11.4 %copy-start = (f32[6,2,128,128]{3,2,1,0:T(8,128)S(1)}, f32[6,2,128,128]{3,2,1,0:T(8,128)}, u32[]{:S(2)}) copy-start(f32[6,2,128,128]{3,2,1,0:T(8,128)} %param.2) | copy-start | bytes 2359300
  100.2 2.0 %collective-permute-start.26 = (f32[768,128]{1,0:T(8,128)S(1)}, f32[768,128]{1,0:T(8,128)S(1)}, u32[]{:S(2)}, u32[]{:S(2)}) collective-permute-start(f32[768,128]{1,0:T(8,128)S(1)} %slice.23), channel_id=1, source_target_pairs={{0,16},{16,0},{1,17},{17,1},{2,18},{18,2},{3,19},{19,3},{4,20},{20... | collective-permute-start | bytes 1179656 | tf_op jit(solution)/shard_map/ppermute | solution.py:56

commit v3 on v2

--- a/solution.py
+++ b/solution.py
@@ -15,7 +15,7 @@
 IDS = 8
 PACKED = 2 * HALF + IDS
 PIECE = HALF + IDS
-UNROLL = 4
+UNROLL = 8
 
 
 def device_id(x, y, z, c):
@@ -286,12 +286,14 @@
     here2 = jnp.where(is_near, in_pair, diagonal)
 
     swapped1 = [send(v, CORE) for v in (up1, down1)]
-    up2, down2, far1, *lefts = lax.optimization_barrier((up2, down2, far1, *lefts))
+    up2, down2, far1, swapped1, lefts = lax.optimization_barrier((up2, down2, far1, swapped1, lefts))
     rights = [up1, down1, up2, down2] + swapped1 + [send(v, CORE) for v in (up2, down2)]
     partial = contract(False, "without", lefts, rights, partner_ids)
-    here1, here2, far1, _ = lax.optimization_barrier((here1, here2, far1, up2))
-    others = [send(v, CORE) for v in (here1, far1, here2)]
-    partial, *others = lax.optimization_barrier((partial, *others))
+    here1, _ = lax.optimization_barrier((here1, up2))
+    other_here1 = send(here1, CORE)
+    here2, far1, _ = lax.optimization_barrier((here2, far1, partial))
+    others = [other_here1, send(far1, CORE), send(here2, CORE)]
+    partial, others[0] = lax.optimization_barrier((partial, other_here1))
     partial = contract(False, "only", ends, rights, partner_ids, partial)
     received = send(partial, Y_LO)
 

time: 113 us -> 111 us (0.982)
  Pallas kernels: 20.7 us -> 19 us
    pallas_call x3, Pallas kernels: 19.5 us -> 17.8 us  [contract(): pl.pallas_call(functools.partial(kernel, own_columns, last, start is not...]
  transfers between devices with their start and end apart: 28 -> 28, of which waited for: 10 -> 10; matrix products, arithmetic and copies ran while one was open for 5% -> 5% of each run, Pallas kernels for 17% -> 16%
where the time goes in v3:
time: 111 us; the launch traced here: 110 us
  starting transfers between devices  44.4 us (40%)
  waiting for transfers between devices  39.4 us (35%)
  Pallas kernels  19 us (17%)
  other arithmetic  4.67 us (4%)
  local copies, waits for them, and re-layouts  1.41 us (1%)
    ppermute x28, starting transfers between devices, send(): return lax.ppermute(value, AXES, pairs)  44.4 us
    ppermute x28, waiting for transfers between devices, send(): return lax.ppermute(value, AXES, pairs)  39.4 us
    pallas_call x3, Pallas kernels, contract(): pl.pallas_call(functools.partial(kernel, own_columns, last, start is not...  17.8 us
  transfers between devices with their start and end apart: 28, of which 10 were waited for; matrix products, arithmetic and copies ran while one was open for 5% of the time, Pallas kernels for 16%

profile of v3, /device:TPU:1, one launch (start us, length us, event | category | flops | bytes accessed | tf_op | source)
XLA Modules:
  0.0 109.9 jit_solution(14044319447417615905)
XLA Ops:
  0.6 0.7 convert_element_type.16
  1.5 2.2 %collective-permute-start = (f32[8,128]{1,0:T(8,128)S(1)}, f32[8,128]{1,0:T(8,128)S(1)}, u32[]{:S(2)}, u32[]{:S(2)}) collective-permute-start(f32[8,128]{1,0:T(8,128)S(1)} %pad.4.refs_17_), channel_id=1, source_target_pairs={{0,8},{16,24},{1,9},{17,25},{2,10},{18,26},{3,11},{19,27},{4,12},{... | collective-permute-start | bytes 12296 | tf_op jit(solution)/shard_map/ppermute | solution.py:56
  3.7 1.2 %fusion = (f32[3,2,128,128]{3,2,1,0:T(8,128)S(1)}, f32[3,2,128,128]{3,2,1,0:T(8,128)S(1)}) fusion(f32[6,2,128,128]{3,2,1,0:T(8,128)} %param.2), kind=kLoop, calls=%fused_computation.8 | loop fusion | bytes 1572864 | tf_op jit(solution)/shard_map/slice | solution.py:262
  4.9 1.7 %collective-permute-start.12 = (f32[1544,128]{1,0:T(8,128)S(1)}, f32[1544,128]{1,0:T(8,128)S(1)}, u32[]{:S(2)}, u32[]{:S(2)}) collective-permute-start(f32[1544,128]{1,0:T(8,128)S(1)} %pad_maximum_fusion.refs_0_), channel_id=1, source_target_pairs={{0,1},{16,17},{1,2},{17,18},{2,3},{18,19},{3,4},{19,20},{4,5},{20,... | collective-permute-start | bytes 2371592 | tf_op jit(solution)/shard_map/ppermute | solution.py:56
  6.7 1.2 %collective-permute-start.1 = (f32[1544,128]{1,0:T(8,128)S(1)}, f32[1544,128]{1,0:T(8,128)}, u32[]{:S(2)}, u32[]{:S(2)}) collective-permute-start(f32[1544,128]{1,0:T(8,128)S(1)} %pad_maximum_fusion.refs_0_), channel_id=1, source_target_pairs={{0,64},{16,80},{1,65},{17,81},{2,66},{18,82},{3,67},{19,83},{4,68}... | collective-permute-start | bytes 2371592 | tf_op jit(solution)/shard_map/ppermute | solution.py:56
  7.9 4.5 %collective-permute-start.2 = (f32[1544,128]{1,0:T(8,128)S(1)}, f32[1544,128]{1,0:T(8,128)}, u32[]{:S(2)}, u32[]{:S(2)}) collective-permute-start(f32[1544,128]{1,0:T(8,128)S(1)} %pad_maximum_fusion.refs_0_), channel_id=1, source_target_pairs={{0,32},{16,48},{1,33},{17,49},{2,34},{18,50},{3,35},{19,51},{4,36}... | collective-permute-start | bytes 2371592 | tf_op jit(solution)/shard_map/ppermute | solution.py:56
  12.5 4.2 %collective-permute-start.13 = (f32[1544,128]{1,0:T(8,128)S(1)}, f32[1544,128]{1,0:T(8,128)S(1)}, u32[]{:S(2)}, u32[]{:S(2)}) collective-permute-start(f32[1544,128]{1,0:T(8,128)S(1)} %pad_maximum_fusion.refs_0_), channel_id=1, source_target_pairs={{0,7},{16,23},{1,0},{17,16},{2,1},{18,17},{3,2},{19,18},{4,3},{20,... | collective-permute-start | bytes 2371592 | tf_op jit(solution)/shard_map/ppermute | solution.py:56
  16.7 11.1 %collective-permute-done.12.refs_1_ = f32[1544,128]{1,0:T(8,128)S(1)} collective-permute-done((f32[1544,128]{1,0:T(8,128)S(1)}, f32[1544,128]{1,0:T(8,128)S(1)}, u32[]{:S(2)}, u32[]{:S(2)}) %collective-permute-start.12) | collective-permute-done | bytes 790560 | tf_op jit(solution)/shard_map/ppermute | solution.py:56
  27.7 1.2 %collective-permute-done.2 = f32[1544,128]{1,0:T(8,128)} collective-permute-done((f32[1544,128]{1,0:T(8,128)S(1)}, f32[1544,128]{1,0:T(8,128)}, u32[]{:S(2)}, u32[]{:S(2)}) %collective-permute-start.2) | collective-permute-done | bytes 790560 | tf_op jit(solution)/shard_map/ppermute | solution.py:56
  29.0 2.2 %collective-permute-done.3 = f32[1544,128]{1,0:T(8,128)} collective-permute-done((f32[1544,128]{1,0:T(8,128)S(1)}, f32[1544,128]{1,0:T(8,128)}, u32[]{:S(2)}, u32[]{:S(2)}) %collective-permute-start.3) | collective-permute-done | bytes 790560 | tf_op jit(solution)/shard_map/ppermute | solution.py:56
  31.1 1.4 %broadcast_select_fusion.3 = (f32[1544,128]{1,0:T(8,128)S(1)}, f32[1544,128]{1,0:T(8,128)S(1)}, f32[1544,128]{1,0:T(8,128)S(1)}) fusion(f32[1544,128]{1,0:T(8,128)} %collective-permute-done.3, pred[]{:T(512)S(6)} %eq.9, f32[768,128]{1,0:T(8,128)S(1)} %bitcast.9, f32[8,128]{1,0:T(8,128)S(1)} %pad.4.refs_17_, f32[768,128]{1,0:T(8,128)S(1)} %bitcast.7, ...), kind=kLoop, calls=%fused_computation.4 | loop fusion | flops 988160 | bytes 4743170 | tf_op jit(solution)/shard_map/jit(_where)/select_n | solution.py:285
  32.6 3.6 %collective-permute-start.15 = (f32[1544,128]{1,0:T(8,128)S(1)}, f32[1544,128]{1,0:T(8,128)S(1)}, u32[]{:S(2)}, u32[]{:S(2)}) collective-permute-start(f32[1544,128]{1,0:T(8,128)S(1)} %collective-permute-done.13.refs_2_), channel_id=1, source_target_pairs={{0,7},{16,23},{1,0},{17,16},{2,1},{18,17},{3,2},{19,18},{4,3},{20,... | collective-permute-start | bytes 2371592 | tf_op jit(solution)/shard_map/ppermute | solution.py:56
  36.2 0.8 collective-permute-start.10
  36.9 0.7 collective-permute-start.8
  37.6 9.0 %collective-permute-done.14.refs_3_ = f32[1544,128]{1,0:T(8,128)S(1)} collective-permute-done((f32[1544,128]{1,0:T(8,128)S(1)}, f32[1544,128]{1,0:T(8,128)S(1)}, u32[]{:S(2)}, u32[]{:S(2)}) %collective-permute-start.14) | collective-permute-done | bytes 790560 | tf_op jit(solution)/shard_map/ppermute | solution.py:56
  46.6 1.2 %broadcast_select_fusion.2 = (f32[1544,128]{1,0:T(8,128)S(1)}, f32[1544,128]{1,0:T(8,128)S(1)}) fusion(f32[1544,128]{1,0:T(8,128)} %collective-permute-done.1, f32[1544,128]{1,0:T(8,128)S(1)} %collective-permute-done.4, pred[]{:T(512)S(6)} %eq.9), kind=kLoop, calls=%fused_computation.3 | loop fusion | flops 395264 | bytes 3162113 | tf_op jit(solution)/shard_map/jit(_where)/select_n | solution.py:286
  47.9 4.4 %collective-permute-start.7 = (f32[1544,128]{1,0:T(8,128)}, f32[1544,128]{1,0:T(8,128)S(1)}, u32[]{:S(2)}, u32[]{:S(2)}) collective-permute-start(f32[1544,128]{1,0:T(8,128)} %collective-permute-done.2), channel_id=1, source_target_pairs={{0,192},{16,208},{1,193},{17,209},{2,194},{18,210},{3,195},{19,211... | collective-permute-start | bytes 2371592 | tf_op jit(solution)/shard_map/ppermute | solution.py:56
  52.3 2.7 %collective-permute-start.17 = (f32[1544,128]{1,0:T(8,128)S(1)}, f32[1544,128]{1,0:T(8,128)S(1)}, u32[]{:S(2)}, u32[]{:S(2)}) collective-permute-start(f32[1544,128]{1,0:T(8,128)S(1)} %collective-permute-done.15.refs_4_), channel_id=1, source_target_pairs={{0,7},{16,23},{1,0},{17,16},{2,1},{18,17},{3,2},{19,18},{4,3},{20,... | collective-permute-start | bytes 2371592 | tf_op jit(solution)/shard_map/ppermute | solution.py:56
  55.1 2.7 %collective-permute-start.6 = (f32[1544,128]{1,0:T(8,128)S(1)}, f32[1544,128]{1,0:T(8,128)S(1)}, u32[]{:S(2)}, u32[]{:S(2)}) collective-permute-start(f32[1544,128]{1,0:T(8,128)S(1)} %get-tuple-element.31), channel_id=1, source_target_pairs={{0,40},{16,56},{1,41},{17,57},{2,42},{18,58},{3,43},{19,59},{4,44}... | collective-permute-start | bytes 2371592 | tf_op jit(solution)/shard_map/ppermute | solution.py:56
  57.8 6.8 %collective-permute-done.16.refs_5_ = f32[1544,128]{1,0:T(8,128)S(1)} collective-permute-done((f32[1544,128]{1,0:T(8,128)S(1)}, f32[1544,128]{1,0:T(8,128)S(1)}, u32[]{:S(2)}, u32[]{:S(2)}) %collective-permute-start.16) | collective-permute-done | bytes 790560 | tf_op jit(solution)/shard_map/ppermute | solution.py:56
  64.6 3.3 %collective-permute-start.11 = (f32[1544,128]{1,0:T(8,128)S(1)}, f32[1544,128]{1,0:T(8,128)S(1)}, u32[]{:S(2)}, u32[]{:S(2)}) collective-permute-start(f32[1544,128]{1,0:T(8,128)S(1)} %collective-permute-done.10.refs_8_.refs_2_), channel_id=1, source_target_pairs={{0,16},{16,0},{1,17},{17,1},{2,18},{18,2},{3,19},{19,3},{4,20},{20... | collective-permute-start | bytes 2371592 | tf_op jit(solution)/shard_map/ppermute | solution.py:56
  67.9 2.5 %collective-permute-start.9 = (f32[1544,128]{1,0:T(8,128)S(1)}, f32[1544,128]{1,0:T(8,128)S(1)}, u32[]{:S(2)}, u32[]{:S(2)}) collective-permute-start(f32[1544,128]{1,0:T(8,128)S(1)} %collective-permute-done.8.refs_7_.refs_1_), channel_id=1, source_target_pairs={{0,16},{16,0},{1,17},{17,1},{2,18},{18,2},{3,19},{19,3},{4,20},{20... | collective-permute-start | bytes 2371592 | tf_op jit(solution)/shard_map/ppermute | solution.py:56
  70.4 1.2 %broadcast_select_fusion.5.refs_9_ = f32[1544,128]{1,0:T(8,128)S(1)} fusion(f32[1544,128]{1,0:T(8,128)} %collective-permute-done.2, f32[1544,128]{1,0:T(8,128)S(1)} %collective-permute-done.7, pred[]{:T(512)S(6)} %eq.9), kind=kLoop, calls=%fused_computation.6 | loop fusion | flops 197632 | bytes 2371585 | tf_op jit(solution)/shard_map/jit(_where)/select_n | solution.py:283
  72.3 4.3 %collective-permute-start.19 = (f32[1544,128]{1,0:T(8,128)S(1)}, f32[1544,128]{1,0:T(8,128)S(1)}, u32[]{:S(2)}, u32[]{:S(2)}) collective-permute-start(f32[1544,128]{1,0:T(8,128)S(1)} %collective-permute-done.5.refs_9_.refs_3_), channel_id=1, source_target_pairs={{0,16},{16,0},{1,17},{17,1},{2,18},{18,2},{3,19},{19,3},{4,20},{20... | collective-permute-start | bytes 2371592 | tf_op jit(solution)/shard_map/ppermute | solution.py:56
  77.4 2.6 %collective-permute-start.21 = (f32[1544,128]{1,0:T(8,128)S(1)}, f32[1544,128]{1,0:T(8,128)S(1)}, u32[]{:S(2)}, u32[]{:S(2)}) collective-permute-start(f32[1544,128]{1,0:T(8,128)S(1)} %broadcast_select_fusion.5.refs_9_), channel_id=1, source_target_pairs={{0,64},{16,80},{1,65},{17,81},{2,66},{18,82},{3,67},{19,83},{4,68}... | collective-permute-start | bytes 2371592 | tf_op jit(solution)/shard_map/ppermute | solution.py:56
  80.0 7.5 %shard_map.41.refs_10_ = f32[12,128,128]{2,1,0:T(8,128)S(1)} custom-call(f32[1544,128]{1,0:T(8,128)S(1)} %pad_maximum_fusion.refs_0_, f32[1544,128]{1,0:T(8,128)S(1)} %collective-permute-done.12.refs_1_, f32[1544,128]{1,0:T(8,128)S(1)} %collective-permute-done.13.refs_2_, f32[1544,128]{1,0:T(8,128)S(1)} %collective-permute-done.14.refs_3_, ...), custom_call_target="tpu_custom_call" | custom-call | flops 1000000 | bytes 1000000 | tf_op jit(solution)/shard_map/pallas_call | solution.py:200
  88.5 1.8 %shard_map.42 = f32[12,128,128]{2,1,0:T(8,128)S(1)} custom-call(f32[1544,128]{1,0:T(8,128)S(1)} %collective-permute-done.18.refs_0_.refs_7_, f32[1544,128]{1,0:T(8,128)S(1)} %collective-permute-done.8.refs_7_.refs_1_, f32[1544,128]{1,0:T(8,128)S(1)} %collective-permute-done.10.refs_8_.refs_2_, f32[1544,128]{1,0:T(8,128)S(1)} %collective-permute-done.5.refs_9_.refs_3_, ...), custom_call_target="tpu_custom_call" | custom-call | flops 1000000 | bytes 1000000 | tf_op jit(solution)/shard_map/pallas_call | solution.py:200
  90.3 0.9 collective-permute-start.27
  91.2 6.4 %collective-permute-done.21.refs_11_ = f32[1544,128]{1,0:T(8,128)S(1)} collective-permute-done((f32[1544,128]{1,0:T(8,128)S(1)}, f32[1544,128]{1,0:T(8,128)S(1)}, u32[]{:S(2)}, u32[]{:S(2)}) %collective-permute-start.21) | collective-permute-done | bytes 790560 | tf_op jit(solution)/shard_map/ppermute | solution.py:56
  98.4 1.7 %collective-permute-done.26.refs_16_ = f32[768,128]{1,0:T(8,128)S(1)} collective-permute-done((f32[768,128]{1,0:T(8,128)S(1)}, f32[768,128]{1,0:T(8,128)S(1)}, u32[]{:S(2)}, u32[]{:S(2)}) %collective-permute-start.26) | collective-permute-done | bytes 393248 | tf_op jit(solution)/shard_map/ppermute | solution.py:56
  100.0 8.4 %shard_map.43.mine = f32[12,128,128]{2,1,0:T(8,128)S(1)} custom-call(f32[1544,128]{1,0:T(8,128)S(1)} %pad_maximum_fusion.refs_0_, f32[1544,128]{1,0:T(8,128)S(1)} %collective-permute-done.12.refs_1_, f32[1544,128]{1,0:T(8,128)S(1)} %collective-permute-done.13.refs_2_, f32[1544,128]{1,0:T(8,128)S(1)} %collective-permute-done.14.refs_3_, ...), custom_call_target="tpu_custom_call" | custom-call | flops 1000000 | bytes 1000000 | tf_op jit(solution)/shard_map/pallas_call | solution.py:200
  108.5 1.2 %shard_map.44 = (f32[12,128,128]{2,1,0:T(8,128)}, f32[12,128,128]{2,1,0:T(8,128)}) custom-call(f32[12,128,128]{2,1,0:T(8,128)S(1)} %shard_map.43.mine, f32[12,128,128]{2,1,0:T(8,128)S(1)} %collective-permute-done.27.received, f32[12,128,128]{2,1,0:T(8,128)S(1)} %bitcast.5), custom_call_target="tpu_custom_call" | custom-call | tf_op jit(solution)/shard_map/pallas_call | solution.py:242
  (42 shorter events, 3.6 us)
Async XLA Ops:
  1.5 5.2 %collective-permute-start = (f32[8,128]{1,0:T(8,128)S(1)}, f32[8,128]{1,0:T(8,128)S(1)}, u32[]{:S(2)}, u32[]{:S(2)}) collective-permute-start(f32[8,128]{1,0:T(8,128)S(1)} %pad.4.refs_17_), channel_id=1, source_target_pairs={{0,8},{16,24},{1,9},{17,25},{2,10},{18,26},{3,11},{19,27},{4,12},{... | collective-permute-start | bytes 12296 | tf_op jit(solution)/shard_map/ppermute | solution.py:56
  4.9 22.8 %collective-permute-start.12 = (f32[1544,128]{1,0:T(8,128)S(1)}, f32[1544,128]{1,0:T(8,128)S(1)}, u32[]{:S(2)}, u32[]{:S(2)}) collective-permute-start(f32[1544,128]{1,0:T(8,128)S(1)} %pad_maximum_fusion.refs_0_), channel_id=1, source_target_pairs={{0,1},{16,17},{1,2},{17,18},{2,3},{18,19},{3,4},{19,20},{4,5},{20,... | collective-permute-start | bytes 2371592 | tf_op jit(solution)/shard_map/ppermute | solution.py:56
  6.7 21.1 %collective-permute-start.1 = (f32[1544,128]{1,0:T(8,128)S(1)}, f32[1544,128]{1,0:T(8,128)}, u32[]{:S(2)}, u32[]{:S(2)}) collective-permute-start(f32[1544,128]{1,0:T(8,128)S(1)} %pad_maximum_fusion.refs_0_), channel_id=1, source_target_pairs={{0,64},{16,80},{1,65},{17,81},{2,66},{18,82},{3,67},{19,83},{4,68}... | collective-permute-start | bytes 2371592 | tf_op jit(solution)/shard_map/ppermute | solution.py:56
  7.9 21.1 %collective-permute-start.2 = (f32[1544,128]{1,0:T(8,128)S(1)}, f32[1544,128]{1,0:T(8,128)}, u32[]{:S(2)}, u32[]{:S(2)}) collective-permute-start(f32[1544,128]{1,0:T(8,128)S(1)} %pad_maximum_fusion.refs_0_), channel_id=1, source_target_pairs={{0,32},{16,48},{1,33},{17,49},{2,34},{18,50},{3,35},{19,51},{4,36}... | collective-permute-start | bytes 2371592 | tf_op jit(solution)/shard_map/ppermute | solution.py:56
  12.4 18.7 %collective-permute-start.3 = (f32[1544,128]{1,0:T(8,128)S(1)}, f32[1544,128]{1,0:T(8,128)}, u32[]{:S(2)}, u32[]{:S(2)}) collective-permute-start(f32[1544,128]{1,0:T(8,128)S(1)} %pad_maximum_fusion.refs_0_), channel_id=1, source_target_pairs={{0,192},{16,208},{1,193},{17,209},{2,194},{18,210},{3,195},{19,211... | collective-permute-start | bytes 2371592 | tf_op jit(solution)/shard_map/ppermute | solution.py:56
  12.5 20.1 %collective-permute-start.13 = (f32[1544,128]{1,0:T(8,128)S(1)}, f32[1544,128]{1,0:T(8,128)S(1)}, u32[]{:S(2)}, u32[]{:S(2)}) collective-permute-start(f32[1544,128]{1,0:T(8,128)S(1)} %pad_maximum_fusion.refs_0_), channel_id=1, source_target_pairs={{0,7},{16,23},{1,0},{17,16},{2,1},{18,17},{3,2},{19,18},{4,3},{20,... | collective-permute-start | bytes 2371592 | tf_op jit(solution)/shard_map/ppermute | solution.py:56
  27.7 18.9 %collective-permute-start.14 = (f32[1544,128]{1,0:T(8,128)S(1)}, f32[1544,128]{1,0:T(8,128)S(1)}, u32[]{:S(2)}, u32[]{:S(2)}) collective-permute-start(f32[1544,128]{1,0:T(8,128)S(1)} %collective-permute-done.12.refs_1_), channel_id=1, source_target_pairs={{0,1},{16,17},{1,2},{17,18},{2,3},{18,19},{3,4},{19,20},{4,5},{20,... | collective-permute-start | bytes 2371592 | tf_op jit(solution)/shard_map/ppermute | solution.py:56
  32.5 14.1 %collective-permute-start.4 = (f32[1544,128]{1,0:T(8,128)S(1)}, f32[1544,128]{1,0:T(8,128)S(1)}, u32[]{:S(2)}, u32[]{:S(2)}) collective-permute-start(f32[1544,128]{1,0:T(8,128)S(1)} %get-tuple-element.58), channel_id=1, source_target_pairs={{0,192},{16,80},{1,193},{17,81},{2,194},{18,82},{3,195},{19,83},{4... | collective-permute-start | bytes 2371592 | tf_op jit(solution)/shard_map/ppermute | solution.py:56
  32.6 19.7 %collective-permute-start.15 = (f32[1544,128]{1,0:T(8,128)S(1)}, f32[1544,128]{1,0:T(8,128)S(1)}, u32[]{:S(2)}, u32[]{:S(2)}) collective-permute-start(f32[1544,128]{1,0:T(8,128)S(1)} %collective-permute-done.13.refs_2_), channel_id=1, source_target_pairs={{0,7},{16,23},{1,0},{17,16},{2,1},{18,17},{3,2},{19,18},{4,3},{20,... | collective-permute-start | bytes 2371592 | tf_op jit(solution)/shard_map/ppermute | solution.py:56
  36.2 18.9 %collective-permute-start.10 = (f32[1544,128]{1,0:T(8,128)S(1)}, f32[1544,128]{1,0:T(8,128)S(1)}, u32[]{:S(2)}, u32[]{:S(2)}) collective-permute-start(f32[1544,128]{1,0:T(8,128)S(1)} %get-tuple-element.57), channel_id=1, source_target_pairs={{0,40},{16,56},{1,41},{17,57},{2,42},{18,58},{3,43},{19,59},{4,44}... | collective-permute-start | bytes 2371592 | tf_op jit(solution)/shard_map/ppermute | solution.py:56
  36.9 18.2 %collective-permute-start.8 = (f32[1544,128]{1,0:T(8,128)S(1)}, f32[1544,128]{1,0:T(8,128)S(1)}, u32[]{:S(2)}, u32[]{:S(2)}) collective-permute-start(f32[1544,128]{1,0:T(8,128)S(1)} %get-tuple-element.57), channel_id=1, source_target_pairs={{0,8},{16,24},{1,9},{17,25},{2,10},{18,26},{3,11},{19,27},{4,12},{... | collective-permute-start | bytes 2371592 | tf_op jit(solution)/shard_map/ppermute | solution.py:56
  46.6 18.0 %collective-permute-start.16 = (f32[1544,128]{1,0:T(8,128)S(1)}, f32[1544,128]{1,0:T(8,128)S(1)}, u32[]{:S(2)}, u32[]{:S(2)}) collective-permute-start(f32[1544,128]{1,0:T(8,128)S(1)} %collective-permute-done.14.refs_3_), channel_id=1, source_target_pairs={{0,1},{16,17},{1,2},{17,18},{2,3},{18,19},{3,4},{19,20},{4,5},{20,... | collective-permute-start | bytes 2371592 | tf_op jit(solution)/shard_map/ppermute | solution.py:56
  47.9 20.0 %collective-permute-start.7 = (f32[1544,128]{1,0:T(8,128)}, f32[1544,128]{1,0:T(8,128)S(1)}, u32[]{:S(2)}, u32[]{:S(2)}) collective-permute-start(f32[1544,128]{1,0:T(8,128)} %collective-permute-done.2), channel_id=1, source_target_pairs={{0,192},{16,208},{1,193},{17,209},{2,194},{18,210},{3,195},{19,211... | collective-permute-start | bytes 2371592 | tf_op jit(solution)/shard_map/ppermute | solution.py:56
  52.3 19.3 %collective-permute-start.17 = (f32[1544,128]{1,0:T(8,128)S(1)}, f32[1544,128]{1,0:T(8,128)S(1)}, u32[]{:S(2)}, u32[]{:S(2)}) collective-permute-start(f32[1544,128]{1,0:T(8,128)S(1)} %collective-permute-done.15.refs_4_), channel_id=1, source_target_pairs={{0,7},{16,23},{1,0},{17,16},{2,1},{18,17},{3,2},{19,18},{4,3},{20,... | collective-permute-start | bytes 2371592 | tf_op jit(solution)/shard_map/ppermute | solution.py:56
  55.1 17.1 %collective-permute-start.5 = (f32[1544,128]{1,0:T(8,128)S(1)}, f32[1544,128]{1,0:T(8,128)S(1)}, u32[]{:S(2)}, u32[]{:S(2)}) collective-permute-start(f32[1544,128]{1,0:T(8,128)S(1)} %get-tuple-element.31), channel_id=1, source_target_pairs={{0,8},{16,24},{1,9},{17,25},{2,10},{18,26},{3,11},{19,27},{4,12},{... | collective-permute-start | bytes 2371592 | tf_op jit(solution)/shard_map/ppermute | solution.py:56
  55.1 17.1 %collective-permute-start.6 = (f32[1544,128]{1,0:T(8,128)S(1)}, f32[1544,128]{1,0:T(8,128)S(1)}, u32[]{:S(2)}, u32[]{:S(2)}) collective-permute-start(f32[1544,128]{1,0:T(8,128)S(1)} %get-tuple-element.31), channel_id=1, source_target_pairs={{0,40},{16,56},{1,41},{17,57},{2,42},{18,58},{3,43},{19,59},{4,44}... | collective-permute-start | bytes 2371592 | tf_op jit(solution)/shard_map/ppermute | solution.py:56
  64.6 7.6 %collective-permute-start.11 = (f32[1544,128]{1,0:T(8,128)S(1)}, f32[1544,128]{1,0:T(8,128)S(1)}, u32[]{:S(2)}, u32[]{:S(2)}) collective-permute-start(f32[1544,128]{1,0:T(8,128)S(1)} %collective-permute-done.10.refs_8_.refs_2_), channel_id=1, source_target_pairs={{0,16},{16,0},{1,17},{17,1},{2,18},{18,2},{3,19},{19,3},{4,20},{20... | collective-permute-start | bytes 2371592 | tf_op jit(solution)/shard_map/ppermute | solution.py:56
  67.9 4.4 %collective-permute-start.9 = (f32[1544,128]{1,0:T(8,128)S(1)}, f32[1544,128]{1,0:T(8,128)S(1)}, u32[]{:S(2)}, u32[]{:S(2)}) collective-permute-start(f32[1544,128]{1,0:T(8,128)S(1)} %collective-permute-done.8.refs_7_.refs_1_), channel_id=1, source_target_pairs={{0,16},{16,0},{1,17},{17,1},{2,18},{18,2},{3,19},{19,3},{4,20},{20... | collective-permute-start | bytes 2371592 | tf_op jit(solution)/shard_map/ppermute | solution.py:56
  72.3 7.7 %collective-permute-start.19 = (f32[1544,128]{1,0:T(8,128)S(1)}, f32[1544,128]{1,0:T(8,128)S(1)}, u32[]{:S(2)}, u32[]{:S(2)}) collective-permute-start(f32[1544,128]{1,0:T(8,128)S(1)} %collective-permute-done.5.refs_9_.refs_3_), channel_id=1, source_target_pairs={{0,16},{16,0},{1,17},{17,1},{2,18},{18,2},{3,19},{19,3},{4,20},{20... | collective-permute-start | bytes 2371592 | tf_op jit(solution)/shard_map/ppermute | solution.py:56
  76.6 3.4 %collective-permute-start.20 = (f32[1544,128]{1,0:T(8,128)S(1)}, f32[1544,128]{1,0:T(8,128)S(1)}, u32[]{:S(2)}, u32[]{:S(2)}) collective-permute-start(f32[1544,128]{1,0:T(8,128)S(1)} %collective-permute-done.6.refs_10_.refs_4_), channel_id=1, source_target_pairs={{0,16},{16,0},{1,17},{17,1},{2,18},{18,2},{3,19},{19,3},{4,20},{20... | collective-permute-start | bytes 2371592 | tf_op jit(solution)/shard_map/ppermute | solution.py:56
  76.7 11.4 %collective-permute-start.22 = (f32[1544,128]{1,0:T(8,128)S(1)}, f32[1544,128]{1,0:T(8,128)S(1)}, u32[]{:S(2)}, u32[]{:S(2)}) collective-permute-start(f32[1544,128]{1,0:T(8,128)S(1)} %get-tuple-element.41.refs_8_), channel_id=1, source_target_pairs={{0,16},{16,0},{1,17},{17,1},{2,18},{18,2},{3,19},{19,3},{4,20},{20... | collective-permute-start | bytes 2371592 | tf_op jit(solution)/shard_map/ppermute | solution.py:56
  77.2 11.3 %collective-permute-start.18 = (f32[1544,128]{1,0:T(8,128)S(1)}, f32[1544,128]{1,0:T(8,128)S(1)}, u32[]{:S(2)}, u32[]{:S(2)}) collective-permute-start(f32[1544,128]{1,0:T(8,128)S(1)} %broadcast_select_fusion), channel_id=1, source_target_pairs={{0,1},{16,23},{1,2},{17,16},{2,3},{18,17},{3,4},{19,18},{4,5},{20,... | collective-permute-start | bytes 2371592 | tf_op jit(solution)/shard_map/ppermute | solution.py:56
  77.4 20.2 %collective-permute-start.21 = (f32[1544,128]{1,0:T(8,128)S(1)}, f32[1544,128]{1,0:T(8,128)S(1)}, u32[]{:S(2)}, u32[]{:S(2)}) collective-permute-start(f32[1544,128]{1,0:T(8,128)S(1)} %broadcast_select_fusion.5.refs_9_), channel_id=1, source_target_pairs={{0,64},{16,80},{1,65},{17,81},{2,66},{18,82},{3,67},{19,83},{4,68}... | collective-permute-start | bytes 2371592 | tf_op jit(solution)/shard_map/ppermute | solution.py:56
  87.5 12.5 %collective-permute-start.23 = (f32[1544,128]{1,0:T(8,128)S(1)}, f32[1544,128]{1,0:T(8,128)S(1)}, u32[]{:S(2)}, u32[]{:S(2)}) collective-permute-start(f32[1544,128]{1,0:T(8,128)S(1)} %broadcast_select_fusion.5.refs_9_), channel_id=1, source_target_pairs={{0,16},{16,0},{1,17},{17,1},{2,18},{18,2},{3,19},{19,3},{4,20},{20... | collective-permute-start | bytes 2371592 | tf_op jit(solution)/shard_map/ppermute | solution.py:56
  87.6 12.4 %collective-permute-start.24 = (f32[1544,128]{1,0:T(8,128)S(1)}, f32[1544,128]{1,0:T(8,128)S(1)}, u32[]{:S(2)}, u32[]{:S(2)}) collective-permute-start(f32[1544,128]{1,0:T(8,128)S(1)} %get-tuple-element.48.refs_10_), channel_id=1, source_target_pairs={{0,16},{16,0},{1,17},{17,1},{2,18},{18,2},{3,19},{19,3},{4,20},{20... | collective-permute-start | bytes 2371592 | tf_op jit(solution)/shard_map/ppermute | solution.py:56
  90.3 18.2 %collective-permute-start.27 = (f32[12,128,128]{2,1,0:T(8,128)S(1)}, f32[12,128,128]{2,1,0:T(8,128)S(1)}, u32[]{:S(2)}, u32[]{:S(2)}) collective-permute-start(f32[12,128,128]{2,1,0:T(8,128)S(1)} %shard_map.42), channel_id=1, source_target_pairs={{0,8},{16,24},{1,9},{17,25},{2,10},{18,26},{3,11},{19,27},{4,12},{... | collective-permute-start | bytes 2359304 | tf_op jit(solution)/shard_map/ppermute | solution.py:56
  97.6 2.4 %collective-permute-start.25 = (f32[776,128]{1,0:T(8,128)S(1)}, f32[776,128]{1,0:T(8,128)S(1)}, u32[]{:S(2)}, u32[]{:S(2)}) collective-permute-start(f32[776,128]{1,0:T(8,128)S(1)} %slice.22), channel_id=1, source_target_pairs={{0,16},{16,0},{1,17},{17,1},{2,18},{18,2},{3,19},{19,3},{4,20},{20... | collective-permute-start | bytes 1191944 | tf_op jit(solution)/shard_map/ppermute | solution.py:56
  97.8 10.7 %copy-start = (f32[6,2,128,128]{3,2,1,0:T(8,128)S(1)}, f32[6,2,128,128]{3,2,1,0:T(8,128)}, u32[]{:S(2)}) copy-start(f32[6,2,128,128]{3,2,1,0:T(8,128)} %param.2) | copy-start | bytes 2359300
  97.8 2.2 %collective-permute-start.26 = (f32[768,128]{1,0:T(8,128)S(1)}, f32[768,128]{1,0:T(8,128)S(1)}, u32[]{:S(2)}, u32[]{:S(2)}) collective-permute-start(f32[768,128]{1,0:T(8,128)S(1)} %slice.23), channel_id=1, source_target_pairs={{0,16},{16,0},{1,17},{17,1},{2,18},{18,2},{3,19},{19,3},{4,20},{20... | collective-permute-start | bytes 1179656 | tf_op jit(solution)/shard_map/ppermute | solution.py:56

commit v4 on v3

--- a/solution.py
+++ b/solution.py
@@ -72,7 +72,7 @@
     rights, out_ids, refs = refs[:n_right], refs[n_right], refs[n_right + 1:]
     if started:
         start, refs = refs[0], refs[1:]
-    out, lbuf, rbuf, acc, ids_l, ids_r, ids_o, list_l, list_r, list_o, sem, isem = refs
+    out, lbuf, rbuf, acc, ids_l, ids_r, ids_o, list_l, list_r, list_o, sem, late_sem, isem = refs
     zero_row = (1 if last == "only" else 8) * PACKED
 
     x, y_hi, core, y_lo, z = place()
@@ -102,10 +102,16 @@
     blocks_l = [lax.rem(z + distance + 8, 8) for distance in distances]
     slots_l = [block ^ flip for block in blocks_l]
     copies = [pltpu.make_async_copy(out_ids.at[:, :], ids_o, isem)]
+    late = []
     for n, distance in enumerate(distances):
         copies.append(pltpu.make_async_copy(lefts[n].at[pl.ds(HALF, IDS), :], ids_l.at[n], isem))
         at = n * PACKED
-        copies.append(pltpu.make_async_copy(lefts[n].at[:, :], lbuf.at[pl.ds(at, PACKED), :], sem))
+        copies.append(
+            pltpu.make_async_copy(lefts[n].at[pl.ds(0, PIECE), :], lbuf.at[pl.ds(at, PIECE), :], sem)
+        )
+        late.append(
+            pltpu.make_async_copy(lefts[n].at[pl.ds(PIECE, HALF), :], lbuf.at[pl.ds(at + PIECE, HALF), :], late_sem)
+        )
     if last != "only":
         for n in range(8):
             copies.extend(right_copies(n, right_slot(n)))
@@ -123,6 +129,9 @@
         slots_r = [0]
     else:
         slots_r = slots_l
+
+    for copy in late:
+        copy.start()
 
     rbuf[pl.ds(zero_row, BS), :] = jnp.zeros((BS, BS), jnp.float32)
     if started:
@@ -153,7 +162,8 @@
         list_r[n] = zero_row
         return n + n % 2
 
-    n = lax.fori_loop(0, BLOCKS, list_output, 0)
+    half_n = lax.fori_loop(0, BLOCKS // 2, list_output, 0)
+    n = lax.fori_loop(BLOCKS // 2, BLOCKS, list_output, half_n)
     pairs = n // 2
     for u in range(UNROLL):
         list_o[pairs + u] = BLOCKS
@@ -188,7 +198,11 @@
             acc[o] = acc[o] + results[u]
         return carry
 
-    lax.fori_loop(0, (pairs + UNROLL - 1) // UNROLL, step, 0)
+    early = half_n // (2 * UNROLL)
+    lax.fori_loop(0, early, step, 0)
+    for copy in late:
+        copy.wait()
+    lax.fori_loop(early, (pairs + UNROLL - 1) // UNROLL, step, 0)
     out[...] = acc[:BLOCKS]
 
 
@@ -214,6 +228,7 @@
             pltpu.SMEM((longest // 2 + 1,), jnp.int32),
             pltpu.SemaphoreType.DMA,
             pltpu.SemaphoreType.DMA,
+            pltpu.SemaphoreType.DMA,
         ],
         compiler_params=pltpu.CompilerParams(vmem_limit_bytes=(8 if n == 1 else 30) * 2 ** 20),
         cost_estimate=pl.CostEstimate(flops=10 ** 6, bytes_accessed=10 ** 6, transcendentals=0),

time: 111 us -> 113 us (1.018)
  Pallas kernels: 19 us -> 23 us
  waiting for transfers between devices: 39.4 us -> 37.9 us
    pallas_call x3, Pallas kernels: 17.8 us -> 21.8 us  [contract(): pl.pallas_call(functools.partial(kernel, own_columns, last, start is not...]
    ppermute x28, waiting for transfers between devices: 39.4 us -> 37.9 us  [send(): return lax.ppermute(value, AXES, pairs)]
  transfers between devices with their start and end apart: 28 -> 28, of which waited for: 10 -> 9; matrix products, arithmetic and copies ran while one was open for 5% -> 5% of each run, Pallas kernels for 16% -> 19%
where the time goes in v4:
time: 113 us
  starting transfers between devices  44.5 us (39%)
  waiting for transfers between devices  37.9 us (34%)
  Pallas kernels  23 us (20%)
  other arithmetic  4.67 us (4%)
  local copies, waits for them, and re-layouts  1.41 us (1%)
    ppermute x28, starting transfers between devices, send(): return lax.ppermute(value, AXES, pairs)  44.5 us
    ppermute x28, waiting for transfers between devices, send(): return lax.ppermute(value, AXES, pairs)  37.9 us
    pallas_call x3, Pallas kernels, contract(): pl.pallas_call(functools.partial(kernel, own_columns, last, start is not...  21.8 us
  transfers between devices with their start and end apart: 28, of which 9 were waited for; matrix products, arithmetic and copies ran while one was open for 5% of the time, Pallas kernels for 19%

profile of v4, /device:TPU:1, one launch (start us, length us, event | category | flops | bytes accessed | tf_op | source)
XLA Modules:
  0.0 112.6 jit_solution(8639353063098880366)
XLA Ops:
  0.6 0.7 convert_element_type.16
  1.5 2.2 %collective-permute-start = (f32[8,128]{1,0:T(8,128)S(1)}, f32[8,128]{1,0:T(8,128)S(1)}, u32[]{:S(2)}, u32[]{:S(2)}) collective-permute-start(f32[8,128]{1,0:T(8,128)S(1)} %pad.4.refs_17_), channel_id=1, source_target_pairs={{0,8},{16,24},{1,9},{17,25},{2,10},{18,26},{3,11},{19,27},{4,12},{... | collective-permute-start | bytes 12296 | tf_op jit(solution)/shard_map/ppermute | solution.py:56
  3.7 1.2 %fusion = (f32[3,2,128,128]{3,2,1,0:T(8,128)S(1)}, f32[3,2,128,128]{3,2,1,0:T(8,128)S(1)}) fusion(f32[6,2,128,128]{3,2,1,0:T(8,128)} %param.2), kind=kLoop, calls=%fused_computation.8 | loop fusion | bytes 1572864 | tf_op jit(solution)/shard_map/slice | solution.py:277
  4.9 1.7 %collective-permute-start.12 = (f32[1544,128]{1,0:T(8,128)S(1)}, f32[1544,128]{1,0:T(8,128)S(1)}, u32[]{:S(2)}, u32[]{:S(2)}) collective-permute-start(f32[1544,128]{1,0:T(8,128)S(1)} %pad_maximum_fusion.refs_0_), channel_id=1, source_target_pairs={{0,1},{16,17},{1,2},{17,18},{2,3},{18,19},{3,4},{19,20},{4,5},{20,... | collective-permute-start | bytes 2371592 | tf_op jit(solution)/shard_map/ppermute | solution.py:56
  6.7 1.2 %collective-permute-start.1 = (f32[1544,128]{1,0:T(8,128)S(1)}, f32[1544,128]{1,0:T(8,128)}, u32[]{:S(2)}, u32[]{:S(2)}) collective-permute-start(f32[1544,128]{1,0:T(8,128)S(1)} %pad_maximum_fusion.refs_0_), channel_id=1, source_target_pairs={{0,64},{16,80},{1,65},{17,81},{2,66},{18,82},{3,67},{19,83},{4,68}... | collective-permute-start | bytes 2371592 | tf_op jit(solution)/shard_map/ppermute | solution.py:56
  7.9 4.5 %collective-permute-start.2 = (f32[1544,128]{1,0:T(8,128)S(1)}, f32[1544,128]{1,0:T(8,128)}, u32[]{:S(2)}, u32[]{:S(2)}) collective-permute-start(f32[1544,128]{1,0:T(8,128)S(1)} %pad_maximum_fusion.refs_0_), channel_id=1, source_target_pairs={{0,32},{16,48},{1,33},{17,49},{2,34},{18,50},{3,35},{19,51},{4,36}... | collective-permute-start | bytes 2371592 | tf_op jit(solution)/shard_map/ppermute | solution.py:56
  12.5 4.2 %collective-permute-start.13 = (f32[1544,128]{1,0:T(8,128)S(1)}, f32[1544,128]{1,0:T(8,128)S(1)}, u32[]{:S(2)}, u32[]{:S(2)}) collective-permute-start(f32[1544,128]{1,0:T(8,128)S(1)} %pad_maximum_fusion.refs_0_), channel_id=1, source_target_pairs={{0,7},{16,23},{1,0},{17,16},{2,1},{18,17},{3,2},{19,18},{4,3},{20,... | collective-permute-start | bytes 2371592 | tf_op jit(solution)/shard_map/ppermute | solution.py:56
  16.7 11.1 %collective-permute-done.12.refs_1_ = f32[1544,128]{1,0:T(8,128)S(1)} collective-permute-done((f32[1544,128]{1,0:T(8,128)S(1)}, f32[1544,128]{1,0:T(8,128)S(1)}, u32[]{:S(2)}, u32[]{:S(2)}) %collective-permute-start.12) | collective-permute-done | bytes 790560 | tf_op jit(solution)/shard_map/ppermute | solution.py:56
  27.7 1.2 %collective-permute-done.2 = f32[1544,128]{1,0:T(8,128)} collective-permute-done((f32[1544,128]{1,0:T(8,128)S(1)}, f32[1544,128]{1,0:T(8,128)}, u32[]{:S(2)}, u32[]{:S(2)}) %collective-permute-start.2) | collective-permute-done | bytes 790560 | tf_op jit(solution)/shard_map/ppermute | solution.py:56
  29.0 2.2 %collective-permute-done.3 = f32[1544,128]{1,0:T(8,128)} collective-permute-done((f32[1544,128]{1,0:T(8,128)S(1)}, f32[1544,128]{1,0:T(8,128)}, u32[]{:S(2)}, u32[]{:S(2)}) %collective-permute-start.3) | collective-permute-done | bytes 790560 | tf_op jit(solution)/shard_map/ppermute | solution.py:56
  31.1 1.4 %broadcast_select_fusion.3 = (f32[1544,128]{1,0:T(8,128)S(1)}, f32[1544,128]{1,0:T(8,128)S(1)}, f32[1544,128]{1,0:T(8,128)S(1)}) fusion(f32[1544,128]{1,0:T(8,128)} %collective-permute-done.3, pred[]{:T(512)S(6)} %eq.9, f32[768,128]{1,0:T(8,128)S(1)} %bitcast.9, f32[8,128]{1,0:T(8,128)S(1)} %pad.4.refs_17_, f32[768,128]{1,0:T(8,128)S(1)} %bitcast.7, ...), kind=kLoop, calls=%fused_computation.4 | loop fusion | flops 988160 | bytes 4743170 | tf_op jit(solution)/shard_map/jit(_where)/select_n | solution.py:300
  32.6 3.6 %collective-permute-start.15 = (f32[1544,128]{1,0:T(8,128)S(1)}, f32[1544,128]{1,0:T(8,128)S(1)}, u32[]{:S(2)}, u32[]{:S(2)}) collective-permute-start(f32[1544,128]{1,0:T(8,128)S(1)} %collective-permute-done.13.refs_2_), channel_id=1, source_target_pairs={{0,7},{16,23},{1,0},{17,16},{2,1},{18,17},{3,2},{19,18},{4,3},{20,... | collective-permute-start | bytes 2371592 | tf_op jit(solution)/shard_map/ppermute | solution.py:56
  36.2 0.8 collective-permute-start.10
  36.9 0.7 collective-permute-start.8
  37.6 9.0 %collective-permute-done.14.refs_3_ = f32[1544,128]{1,0:T(8,128)S(1)} collective-permute-done((f32[1544,128]{1,0:T(8,128)S(1)}, f32[1544,128]{1,0:T(8,128)S(1)}, u32[]{:S(2)}, u32[]{:S(2)}) %collective-permute-start.14) | collective-permute-done | bytes 790560 | tf_op jit(solution)/shard_map/ppermute | solution.py:56
  46.6 1.2 %broadcast_select_fusion.2 = (f32[1544,128]{1,0:T(8,128)S(1)}, f32[1544,128]{1,0:T(8,128)S(1)}) fusion(f32[1544,128]{1,0:T(8,128)} %collective-permute-done.1, f32[1544,128]{1,0:T(8,128)S(1)} %collective-permute-done.4, pred[]{:T(512)S(6)} %eq.9), kind=kLoop, calls=%fused_computation.3 | loop fusion | flops 395264 | bytes 3162113 | tf_op jit(solution)/shard_map/jit(_where)/select_n | solution.py:301
  47.9 4.4 %collective-permute-start.7 = (f32[1544,128]{1,0:T(8,128)}, f32[1544,128]{1,0:T(8,128)S(1)}, u32[]{:S(2)}, u32[]{:S(2)}) collective-permute-start(f32[1544,128]{1,0:T(8,128)} %collective-permute-done.2), channel_id=1, source_target_pairs={{0,192},{16,208},{1,193},{17,209},{2,194},{18,210},{3,195},{19,211... | collective-permute-start | bytes 2371592 | tf_op jit(solution)/shard_map/ppermute | solution.py:56
  52.3 2.7 %collective-permute-start.17 = (f32[1544,128]{1,0:T(8,128)S(1)}, f32[1544,128]{1,0:T(8,128)S(1)}, u32[]{:S(2)}, u32[]{:S(2)}) collective-permute-start(f32[1544,128]{1,0:T(8,128)S(1)} %collective-permute-done.15.refs_4_), channel_id=1, source_target_pairs={{0,7},{16,23},{1,0},{17,16},{2,1},{18,17},{3,2},{19,18},{4,3},{20,... | collective-permute-start | bytes 2371592 | tf_op jit(solution)/shard_map/ppermute | solution.py:56
  55.1 2.7 %collective-permute-start.6 = (f32[1544,128]{1,0:T(8,128)S(1)}, f32[1544,128]{1,0:T(8,128)S(1)}, u32[]{:S(2)}, u32[]{:S(2)}) collective-permute-start(f32[1544,128]{1,0:T(8,128)S(1)} %get-tuple-element.31), channel_id=1, source_target_pairs={{0,40},{16,56},{1,41},{17,57},{2,42},{18,58},{3,43},{19,59},{4,44}... | collective-permute-start | bytes 2371592 | tf_op jit(solution)/shard_map/ppermute | solution.py:56
  57.8 6.8 %collective-permute-done.16.refs_5_ = f32[1544,128]{1,0:T(8,128)S(1)} collective-permute-done((f32[1544,128]{1,0:T(8,128)S(1)}, f32[1544,128]{1,0:T(8,128)S(1)}, u32[]{:S(2)}, u32[]{:S(2)}) %collective-permute-start.16) | collective-permute-done | bytes 790560 | tf_op jit(solution)/shard_map/ppermute | solution.py:56
  64.6 3.3 %collective-permute-start.11 = (f32[1544,128]{1,0:T(8,128)S(1)}, f32[1544,128]{1,0:T(8,128)S(1)}, u32[]{:S(2)}, u32[]{:S(2)}) collective-permute-start(f32[1544,128]{1,0:T(8,128)S(1)} %collective-permute-done.10.refs_8_.refs_2_), channel_id=1, source_target_pairs={{0,16},{16,0},{1,17},{17,1},{2,18},{18,2},{3,19},{19,3},{4,20},{20... | collective-permute-start | bytes 2371592 | tf_op jit(solution)/shard_map/ppermute | solution.py:56
  67.9 2.5 %collective-permute-start.9 = (f32[1544,128]{1,0:T(8,128)S(1)}, f32[1544,128]{1,0:T(8,128)S(1)}, u32[]{:S(2)}, u32[]{:S(2)}) collective-permute-start(f32[1544,128]{1,0:T(8,128)S(1)} %collective-permute-done.8.refs_7_.refs_1_), channel_id=1, source_target_pairs={{0,16},{16,0},{1,17},{17,1},{2,18},{18,2},{3,19},{19,3},{4,20},{20... | collective-permute-start | bytes 2371592 | tf_op jit(solution)/shard_map/ppermute | solution.py:56
  70.4 1.2 %broadcast_select_fusion.5.refs_9_ = f32[1544,128]{1,0:T(8,128)S(1)} fusion(f32[1544,128]{1,0:T(8,128)} %collective-permute-done.2, f32[1544,128]{1,0:T(8,128)S(1)} %collective-permute-done.7, pred[]{:T(512)S(6)} %eq.9), kind=kLoop, calls=%fused_computation.6 | loop fusion | flops 197632 | bytes 2371585 | tf_op jit(solution)/shard_map/jit(_where)/select_n | solution.py:298
  72.3 4.3 %collective-permute-start.19 = (f32[1544,128]{1,0:T(8,128)S(1)}, f32[1544,128]{1,0:T(8,128)S(1)}, u32[]{:S(2)}, u32[]{:S(2)}) collective-permute-start(f32[1544,128]{1,0:T(8,128)S(1)} %collective-permute-done.5.refs_9_.refs_3_), channel_id=1, source_target_pairs={{0,16},{16,0},{1,17},{17,1},{2,18},{18,2},{3,19},{19,3},{4,20},{20... | collective-permute-start | bytes 2371592 | tf_op jit(solution)/shard_map/ppermute | solution.py:56
  77.4 2.6 %collective-permute-start.21 = (f32[1544,128]{1,0:T(8,128)S(1)}, f32[1544,128]{1,0:T(8,128)S(1)}, u32[]{:S(2)}, u32[]{:S(2)}) collective-permute-start(f32[1544,128]{1,0:T(8,128)S(1)} %broadcast_select_fusion.5.refs_9_), channel_id=1, source_target_pairs={{0,64},{16,80},{1,65},{17,81},{2,66},{18,82},{3,67},{19,83},{4,68}... | collective-permute-start | bytes 2371592 | tf_op jit(solution)/shard_map/ppermute | solution.py:56
  80.0 8.7 %shard_map.41.refs_10_ = f32[12,128,128]{2,1,0:T(8,128)S(1)} custom-call(f32[1544,128]{1,0:T(8,128)S(1)} %pad_maximum_fusion.refs_0_, f32[1544,128]{1,0:T(8,128)S(1)} %collective-permute-done.12.refs_1_, f32[1544,128]{1,0:T(8,128)S(1)} %collective-permute-done.13.refs_2_, f32[1544,128]{1,0:T(8,128)S(1)} %collective-permute-done.14.refs_3_, ...), custom_call_target="tpu_custom_call" | custom-call | flops 1000000 | bytes 1000000 | tf_op jit(solution)/shard_map/pallas_call | solution.py:214
  89.5 2.0 %shard_map.42 = f32[12,128,128]{2,1,0:T(8,128)S(1)} custom-call(f32[1544,128]{1,0:T(8,128)S(1)} %collective-permute-done.18.refs_0_.refs_7_, f32[1544,128]{1,0:T(8,128)S(1)} %collective-permute-done.8.refs_7_.refs_1_, f32[1544,128]{1,0:T(8,128)S(1)} %collective-permute-done.10.refs_8_.refs_2_, f32[1544,128]{1,0:T(8,128)S(1)} %collective-permute-done.5.refs_9_.refs_3_, ...), custom_call_target="tpu_custom_call" | custom-call | flops 1000000 | bytes 1000000 | tf_op jit(solution)/shard_map/pallas_call | solution.py:214
  91.4 0.9 collective-permute-start.27
  92.3 5.3 %collective-permute-done.21.refs_11_ = f32[1544,128]{1,0:T(8,128)S(1)} collective-permute-done((f32[1544,128]{1,0:T(8,128)S(1)}, f32[1544,128]{1,0:T(8,128)S(1)}, u32[]{:S(2)}, u32[]{:S(2)}) %collective-permute-start.21) | collective-permute-done | bytes 790560 | tf_op jit(solution)/shard_map/ppermute | solution.py:56
  98.4 1.7 %collective-permute-done.26.refs_16_ = f32[768,128]{1,0:T(8,128)S(1)} collective-permute-done((f32[768,128]{1,0:T(8,128)S(1)}, f32[768,128]{1,0:T(8,128)S(1)}, u32[]{:S(2)}, u32[]{:S(2)}) %collective-permute-start.26) | collective-permute-done | bytes 393248 | tf_op jit(solution)/shard_map/ppermute | solution.py:56
  100.0 11.1 %shard_map.43.mine = f32[12,128,128]{2,1,0:T(8,128)S(1)} custom-call(f32[1544,128]{1,0:T(8,128)S(1)} %pad_maximum_fusion.refs_0_, f32[1544,128]{1,0:T(8,128)S(1)} %collective-permute-done.12.refs_1_, f32[1544,128]{1,0:T(8,128)S(1)} %collective-permute-done.13.refs_2_, f32[1544,128]{1,0:T(8,128)S(1)} %collective-permute-done.14.refs_3_, ...), custom_call_target="tpu_custom_call" | custom-call | flops 1000000 | bytes 1000000 | tf_op jit(solution)/shard_map/pallas_call | solution.py:214
  111.2 1.2 %shard_map.44 = (f32[12,128,128]{2,1,0:T(8,128)}, f32[12,128,128]{2,1,0:T(8,128)}) custom-call(f32[12,128,128]{2,1,0:T(8,128)S(1)} %shard_map.43.mine, f32[12,128,128]{2,1,0:T(8,128)S(1)} %collective-permute-done.27.received, f32[12,128,128]{2,1,0:T(8,128)S(1)} %bitcast.5), custom_call_target="tpu_custom_call" | custom-call | tf_op jit(solution)/shard_map/pallas_call | solution.py:257
  (42 shorter events, 3.4 us)
Async XLA Ops:
  1.5 5.2 %collective-permute-start = (f32[8,128]{1,0:T(8,128)S(1)}, f32[8,128]{1,0:T(8,128)S(1)}, u32[]{:S(2)}, u32[]{:S(2)}) collective-permute-start(f32[8,128]{1,0:T(8,128)S(1)} %pad.4.refs_17_), channel_id=1, source_target_pairs={{0,8},{16,24},{1,9},{17,25},{2,10},{18,26},{3,11},{19,27},{4,12},{... | collective-permute-start | bytes 12296 | tf_op jit(solution)/shard_map/ppermute | solution.py:56
  4.9 22.8 %collective-permute-start.12 = (f32[1544,128]{1,0:T(8,128)S(1)}, f32[1544,128]{1,0:T(8,128)S(1)}, u32[]{:S(2)}, u32[]{:S(2)}) collective-permute-start(f32[1544,128]{1,0:T(8,128)S(1)} %pad_maximum_fusion.refs_0_), channel_id=1, source_target_pairs={{0,1},{16,17},{1,2},{17,18},{2,3},{18,19},{3,4},{19,20},{4,5},{20,... | collective-permute-start | bytes 2371592 | tf_op jit(solution)/shard_map/ppermute | solution.py:56
  6.7 21.1 %collective-permute-start.1 = (f32[1544,128]{1,0:T(8,128)S(1)}, f32[1544,128]{1,0:T(8,128)}, u32[]{:S(2)}, u32[]{:S(2)}) collective-permute-start(f32[1544,128]{1,0:T(8,128)S(1)} %pad_maximum_fusion.refs_0_), channel_id=1, source_target_pairs={{0,64},{16,80},{1,65},{17,81},{2,66},{18,82},{3,67},{19,83},{4,68}... | collective-permute-start | bytes 2371592 | tf_op jit(solution)/shard_map/ppermute | solution.py:56
  7.9 21.1 %collective-permute-start.2 = (f32[1544,128]{1,0:T(8,128)S(1)}, f32[1544,128]{1,0:T(8,128)}, u32[]{:S(2)}, u32[]{:S(2)}) collective-permute-start(f32[1544,128]{1,0:T(8,128)S(1)} %pad_maximum_fusion.refs_0_), channel_id=1, source_target_pairs={{0,32},{16,48},{1,33},{17,49},{2,34},{18,50},{3,35},{19,51},{4,36}... | collective-permute-start | bytes 2371592 | tf_op jit(solution)/shard_map/ppermute | solution.py:56
  12.4 18.7 %collective-permute-start.3 = (f32[1544,128]{1,0:T(8,128)S(1)}, f32[1544,128]{1,0:T(8,128)}, u32[]{:S(2)}, u32[]{:S(2)}) collective-permute-start(f32[1544,128]{1,0:T(8,128)S(1)} %pad_maximum_fusion.refs_0_), channel_id=1, source_target_pairs={{0,192},{16,208},{1,193},{17,209},{2,194},{18,210},{3,195},{19,211... | collective-permute-start | bytes 2371592 | tf_op jit(solution)/shard_map/ppermute | solution.py:56
  12.5 20.1 %collective-permute-start.13 = (f32[1544,128]{1,0:T(8,128)S(1)}, f32[1544,128]{1,0:T(8,128)S(1)}, u32[]{:S(2)}, u32[]{:S(2)}) collective-permute-start(f32[1544,128]{1,0:T(8,128)S(1)} %pad_maximum_fusion.refs_0_), channel_id=1, source_target_pairs={{0,7},{16,23},{1,0},{17,16},{2,1},{18,17},{3,2},{19,18},{4,3},{20,... | collective-permute-start | bytes 2371592 | tf_op jit(solution)/shard_map/ppermute | solution.py:56
  27.7 18.9 %collective-permute-start.14 = (f32[1544,128]{1,0:T(8,128)S(1)}, f32[1544,128]{1,0:T(8,128)S(1)}, u32[]{:S(2)}, u32[]{:S(2)}) collective-permute-start(f32[1544,128]{1,0:T(8,128)S(1)} %collective-permute-done.12.refs_1_), channel_id=1, source_target_pairs={{0,1},{16,17},{1,2},{17,18},{2,3},{18,19},{3,4},{19,20},{4,5},{20,... | collective-permute-start | bytes 2371592 | tf_op jit(solution)/shard_map/ppermute | solution.py:56
  32.5 14.1 %collective-permute-start.4 = (f32[1544,128]{1,0:T(8,128)S(1)}, f32[1544,128]{1,0:T(8,128)S(1)}, u32[]{:S(2)}, u32[]{:S(2)}) collective-permute-start(f32[1544,128]{1,0:T(8,128)S(1)} %get-tuple-element.58), channel_id=1, source_target_pairs={{0,192},{16,80},{1,193},{17,81},{2,194},{18,82},{3,195},{19,83},{4... | collective-permute-start | bytes 2371592 | tf_op jit(solution)/shard_map/ppermute | solution.py:56
  32.6 19.7 %collective-permute-start.15 = (f32[1544,128]{1,0:T(8,128)S(1)}, f32[1544,128]{1,0:T(8,128)S(1)}, u32[]{:S(2)}, u32[]{:S(2)}) collective-permute-start(f32[1544,128]{1,0:T(8,128)S(1)} %collective-permute-done.13.refs_2_), channel_id=1, source_target_pairs={{0,7},{16,23},{1,0},{17,16},{2,1},{18,17},{3,2},{19,18},{4,3},{20,... | collective-permute-start | bytes 2371592 | tf_op jit(solution)/shard_map/ppermute | solution.py:56
  36.2 18.9 %collective-permute-start.10 = (f32[1544,128]{1,0:T(8,128)S(1)}, f32[1544,128]{1,0:T(8,128)S(1)}, u32[]{:S(2)}, u32[]{:S(2)}) collective-permute-start(f32[1544,128]{1,0:T(8,128)S(1)} %get-tuple-element.57), channel_id=1, source_target_pairs={{0,40},{16,56},{1,41},{17,57},{2,42},{18,58},{3,43},{19,59},{4,44}... | collective-permute-start | bytes 2371592 | tf_op jit(solution)/shard_map/ppermute | solution.py:56
  36.9 18.2 %collective-permute-start.8 = (f32[1544,128]{1,0:T(8,128)S(1)}, f32[1544,128]{1,0:T(8,128)S(1)}, u32[]{:S(2)}, u32[]{:S(2)}) collective-permute-start(f32[1544,128]{1,0:T(8,128)S(1)} %get-tuple-element.57), channel_id=1, source_target_pairs={{0,8},{16,24},{1,9},{17,25},{2,10},{18,26},{3,11},{19,27},{4,12},{... | collective-permute-start | bytes 2371592 | tf_op jit(solution)/shard_map/ppermute | solution.py:56
  46.6 18.0 %collective-permute-start.16 = (f32[1544,128]{1,0:T(8,128)S(1)}, f32[1544,128]{1,0:T(8,128)S(1)}, u32[]{:S(2)}, u32[]{:S(2)}) collective-permute-start(f32[1544,128]{1,0:T(8,128)S(1)} %collective-permute-done.14.refs_3_), channel_id=1, source_target_pairs={{0,1},{16,17},{1,2},{17,18},{2,3},{18,19},{3,4},{19,20},{4,5},{20,... | collective-permute-start | bytes 2371592 | tf_op jit(solution)/shard_map/ppermute | solution.py:56
  47.9 20.0 %collective-permute-start.7 = (f32[1544,128]{1,0:T(8,128)}, f32[1544,128]{1,0:T(8,128)S(1)}, u32[]{:S(2)}, u32[]{:S(2)}) collective-permute-start(f32[1544,128]{1,0:T(8,128)} %collective-permute-done.2), channel_id=1, source_target_pairs={{0,192},{16,208},{1,193},{17,209},{2,194},{18,210},{3,195},{19,211... | collective-permute-start | bytes 2371592 | tf_op jit(solution)/shard_map/ppermute | solution.py:56
  52.3 19.3 %collective-permute-start.17 = (f32[1544,128]{1,0:T(8,128)S(1)}, f32[1544,128]{1,0:T(8,128)S(1)}, u32[]{:S(2)}, u32[]{:S(2)}) collective-permute-start(f32[1544,128]{1,0:T(8,128)S(1)} %collective-permute-done.15.refs_4_), channel_id=1, source_target_pairs={{0,7},{16,23},{1,0},{17,16},{2,1},{18,17},{3,2},{19,18},{4,3},{20,... | collective-permute-start | bytes 2371592 | tf_op jit(solution)/shard_map/ppermute | solution.py:56
  55.1 17.1 %collective-permute-start.5 = (f32[1544,128]{1,0:T(8,128)S(1)}, f32[1544,128]{1,0:T(8,128)S(1)}, u32[]{:S(2)}, u32[]{:S(2)}) collective-permute-start(f32[1544,128]{1,0:T(8,128)S(1)} %get-tuple-element.31), channel_id=1, source_target_pairs={{0,8},{16,24},{1,9},{17,25},{2,10},{18,26},{3,11},{19,27},{4,12},{... | collective-permute-start | bytes 2371592 | tf_op jit(solution)/shard_map/ppermute | solution.py:56
  55.1 17.1 %collective-permute-start.6 = (f32[1544,128]{1,0:T(8,128)S(1)}, f32[1544,128]{1,0:T(8,128)S(1)}, u32[]{:S(2)}, u32[]{:S(2)}) collective-permute-start(f32[1544,128]{1,0:T(8,128)S(1)} %get-tuple-element.31), channel_id=1, source_target_pairs={{0,40},{16,56},{1,41},{17,57},{2,42},{18,58},{3,43},{19,59},{4,44}... | collective-permute-start | bytes 2371592 | tf_op jit(solution)/shard_map/ppermute | solution.py:56
  64.6 7.6 %collective-permute-start.11 = (f32[1544,128]{1,0:T(8,128)S(1)}, f32[1544,128]{1,0:T(8,128)S(1)}, u32[]{:S(2)}, u32[]{:S(2)}) collective-permute-start(f32[1544,128]{1,0:T(8,128)S(1)} %collective-permute-done.10.refs_8_.refs_2_), channel_id=1, source_target_pairs={{0,16},{16,0},{1,17},{17,1},{2,18},{18,2},{3,19},{19,3},{4,20},{20... | collective-permute-start | bytes 2371592 | tf_op jit(solution)/shard_map/ppermute | solution.py:56
  67.9 4.4 %collective-permute-start.9 = (f32[1544,128]{1,0:T(8,128)S(1)}, f32[1544,128]{1,0:T(8,128)S(1)}, u32[]{:S(2)}, u32[]{:S(2)}) collective-permute-start(f32[1544,128]{1,0:T(8,128)S(1)} %collective-permute-done.8.refs_7_.refs_1_), channel_id=1, source_target_pairs={{0,16},{16,0},{1,17},{17,1},{2,18},{18,2},{3,19},{19,3},{4,20},{20... | collective-permute-start | bytes 2371592 | tf_op jit(solution)/shard_map/ppermute | solution.py:56
  72.3 7.7 %collective-permute-start.19 = (f32[1544,128]{1,0:T(8,128)S(1)}, f32[1544,128]{1,0:T(8,128)S(1)}, u32[]{:S(2)}, u32[]{:S(2)}) collective-permute-start(f32[1544,128]{1,0:T(8,128)S(1)} %collective-permute-done.5.refs_9_.refs_3_), channel_id=1, source_target_pairs={{0,16},{16,0},{1,17},{17,1},{2,18},{18,2},{3,19},{19,3},{4,20},{20... | collective-permute-start | bytes 2371592 | tf_op jit(solution)/shard_map/ppermute | solution.py:56
  76.6 3.4 %collective-permute-start.20 = (f32[1544,128]{1,0:T(8,128)S(1)}, f32[1544,128]{1,0:T(8,128)S(1)}, u32[]{:S(2)}, u32[]{:S(2)}) collective-permute-start(f32[1544,128]{1,0:T(8,128)S(1)} %collective-permute-done.6.refs_10_.refs_4_), channel_id=1, source_target_pairs={{0,16},{16,0},{1,17},{17,1},{2,18},{18,2},{3,19},{19,3},{4,20},{20... | collective-permute-start | bytes 2371592 | tf_op jit(solution)/shard_map/ppermute | solution.py:56
  76.7 12.7 %collective-permute-start.22 = (f32[1544,128]{1,0:T(8,128)S(1)}, f32[1544,128]{1,0:T(8,128)S(1)}, u32[]{:S(2)}, u32[]{:S(2)}) collective-permute-start(f32[1544,128]{1,0:T(8,128)S(1)} %get-tuple-element.41.refs_8_), channel_id=1, source_target_pairs={{0,16},{16,0},{1,17},{17,1},{2,18},{18,2},{3,19},{19,3},{4,20},{20... | collective-permute-start | bytes 2371592 | tf_op jit(solution)/shard_map/ppermute | solution.py:56
  77.2 12.2 %collective-permute-start.18 = (f32[1544,128]{1,0:T(8,128)S(1)}, f32[1544,128]{1,0:T(8,128)S(1)}, u32[]{:S(2)}, u32[]{:S(2)}) collective-permute-start(f32[1544,128]{1,0:T(8,128)S(1)} %broadcast_select_fusion), channel_id=1, source_target_pairs={{0,1},{16,23},{1,2},{17,16},{2,3},{18,17},{3,4},{19,18},{4,5},{20,... | collective-permute-start | bytes 2371592 | tf_op jit(solution)/shard_map/ppermute | solution.py:56
  77.4 20.2 %collective-permute-start.21 = (f32[1544,128]{1,0:T(8,128)S(1)}, f32[1544,128]{1,0:T(8,128)S(1)}, u32[]{:S(2)}, u32[]{:S(2)}) collective-permute-start(f32[1544,128]{1,0:T(8,128)S(1)} %broadcast_select_fusion.5.refs_9_), channel_id=1, source_target_pairs={{0,64},{16,80},{1,65},{17,81},{2,66},{18,82},{3,67},{19,83},{4,68}... | collective-permute-start | bytes 2371592 | tf_op jit(solution)/shard_map/ppermute | solution.py:56
  88.8 11.3 %collective-permute-start.23 = (f32[1544,128]{1,0:T(8,128)S(1)}, f32[1544,128]{1,0:T(8,128)S(1)}, u32[]{:S(2)}, u32[]{:S(2)}) collective-permute-start(f32[1544,128]{1,0:T(8,128)S(1)} %broadcast_select_fusion.5.refs_9_), channel_id=1, source_target_pairs={{0,16},{16,0},{1,17},{17,1},{2,18},{18,2},{3,19},{19,3},{4,20},{20... | collective-permute-start | bytes 2371592 | tf_op jit(solution)/shard_map/ppermute | solution.py:56
  89.4 10.7 %collective-permute-start.24 = (f32[1544,128]{1,0:T(8,128)S(1)}, f32[1544,128]{1,0:T(8,128)S(1)}, u32[]{:S(2)}, u32[]{:S(2)}) collective-permute-start(f32[1544,128]{1,0:T(8,128)S(1)} %get-tuple-element.48.refs_10_), channel_id=1, source_target_pairs={{0,16},{16,0},{1,17},{17,1},{2,18},{18,2},{3,19},{19,3},{4,20},{20... | collective-permute-start | bytes 2371592 | tf_op jit(solution)/shard_map/ppermute | solution.py:56
  91.4 19.7 %collective-permute-start.27 = (f32[12,128,128]{2,1,0:T(8,128)S(1)}, f32[12,128,128]{2,1,0:T(8,128)S(1)}, u32[]{:S(2)}, u32[]{:S(2)}) collective-permute-start(f32[12,128,128]{2,1,0:T(8,128)S(1)} %shard_map.42), channel_id=1, source_target_pairs={{0,8},{16,24},{1,9},{17,25},{2,10},{18,26},{3,11},{19,27},{4,12},{... | collective-permute-start | bytes 2359304 | tf_op jit(solution)/shard_map/ppermute | solution.py:56
  97.6 2.4 %collective-permute-start.25 = (f32[776,128]{1,0:T(8,128)S(1)}, f32[776,128]{1,0:T(8,128)S(1)}, u32[]{:S(2)}, u32[]{:S(2)}) collective-permute-start(f32[776,128]{1,0:T(8,128)S(1)} %slice.22), channel_id=1, source_target_pairs={{0,16},{16,0},{1,17},{17,1},{2,18},{18,2},{3,19},{19,3},{4,20},{20... | collective-permute-start | bytes 1191944 | tf_op jit(solution)/shard_map/ppermute | solution.py:56
  97.8 13.4 %copy-start = (f32[6,2,128,128]{3,2,1,0:T(8,128)S(1)}, f32[6,2,128,128]{3,2,1,0:T(8,128)}, u32[]{:S(2)}) copy-start(f32[6,2,128,128]{3,2,1,0:T(8,128)} %param.2) | copy-start | bytes 2359300
  97.8 2.2 %collective-permute-start.26 = (f32[768,128]{1,0:T(8,128)S(1)}, f32[768,128]{1,0:T(8,128)S(1)}, u32[]{:S(2)}, u32[]{:S(2)}) collective-permute-start(f32[768,128]{1,0:T(8,128)S(1)} %slice.23), channel_id=1, source_target_pairs={{0,16},{16,0},{1,17},{17,1},{2,18},{18,2},{3,19},{19,3},{4,20},{20... | collective-permute-start | bytes 1179656 | tf_op jit(solution)/shard_map/ppermute | solution.py:56
